TPU v7x, 32 devices: a whole 2x2x4 slice. The times are simulated.
32 devices in a mesh: dp: 4 (over z), mp: 8 (over y, x, core).
Axes of the slice: x: 2, y: 2, z: 4, core: 2. Of those that a mesh axis runs over, the one named last changes fastest.
Arguments:
- inputs: bfloat16 [2, 37632, 1024], P(None, ('dp', 'mp')), may hold values from -6 to 6
- norm0_gain: float32 [1024], replicated, may hold values from 0.5 to 1.5
- norm0_bias: float32 [1024], replicated, may hold values from -1.75 to 1.75
- merge_weight: bfloat16 [1024, 512], replicated, may hold values from -0.1875 to 0.1875
- norm1_gain: float32 [512], replicated, may hold values from 0.5 to 1.5
- norm1_bias: float32 [512], replicated, may hold values from -1.75 to 1.75
- qkv_weight: bfloat16 [512, 16, 96], P(None, 'mp'), may hold values from -0.25 to 0.25
- qkv_bias: bfloat16 [16, 96], P('mp'), may hold values from -1.75 to 1.75
- rel_table: bfloat16 [16, 169], P('mp'), may hold values from -4 to 4
- rel_index: int32 [49, 49], replicated, may hold values from 0 to 168
- regions: int32 [2, 37632], P(None, 'dp'), may hold values from 0 to 3, as said below
- live_windows: int32 [2, 4], P(None, 'dp'), may hold values from 96 to 192, as said below
- proj_weight: bfloat16 [16, 32, 512], P('mp'), may hold values from -0.75 to 0.75
- proj_bias: float32 [512], replicated, may hold values from -1.75 to 1.75
- norm2_gain: float32 [512], replicated, may hold values from 0.5 to 1.5
- norm2_bias: float32 [512], replicated, may hold values from -1.75 to 1.75
- up_weight: bfloat16 [512, 2048], P(None, 'mp'), may hold values from -0.25 to 0.25
- up_bias: bfloat16 [2048], P('mp'), may hold values from -1.75 to 1.75
- down_weight: bfloat16 [2048, 512], P('mp'), may hold values from -0.125 to 0.125
- down_bias: float32 [512], replicated, may hold values from -1.75 to 1.75
- cotangent: bfloat16 [2, 37632, 512], P(None, ('dp', 'mp')), may hold values from -6 to 6
Outputs:
- output: float32 [2, 37632, 512], P(None, ('dp', 'mp'))
- grad_input: float32 [2, 37632, 1024], P(None, ('dp', 'mp'))
- grad_norm0_gain: float32 [1024], replicated
- grad_norm0_bias: float32 [1024], replicated
- grad_merge: float32 [1024, 512], replicated
- grad_norm1_gain: float32 [512], replicated
- grad_norm1_bias: float32 [512], replicated
- grad_qkv: float32 [512, 16, 96], P(None, 'mp')
- grad_qkv_bias: float32 [16, 96], P('mp')
- grad_rel_table: float32 [16, 169], P('mp')
- grad_proj: float32 [16, 32, 512], P('mp')
- grad_proj_bias: float32 [512], replicated
- grad_norm2_gain: float32 [512], replicated
- grad_norm2_bias: float32 [512], replicated
- grad_up: float32 [512, 2048], P(None, 'mp')
- grad_up_bias: float32 [2048], P('mp')
- grad_down: float32 [2048, 512], P('mp')
- grad_down_bias: float32 [512], replicated
Inputs may be any that keep to these rules, and one draw needn't show every extreme that they name: `regions`: in every window the region ids of its positions are 2 * (row >= r) + (column >= c) for that window's cuts r, c from 0 to 6; the first window of each micro-batch is cut both ways. `live_windows`: for every page group some micro-batch has all 192 windows live; live windows are the first ones of their group.
All inputs are finite; a program needn't handle non-finite values.
Results may differ from a plain program's by a relative error of at most 0.018.
Values may be sent and summed in bfloat16 or wider, within the bound.
A program may use at most 256 MiB of HBM per device.

v0:
```python
import math

import jax
import jax.numpy as jnp
from jax import lax
from jax.sharding import PartitionSpec as P

EPSILON = 1e-05
MASKED = -1e30
HIGHEST = lax.Precision.HIGHEST


def normalize(values):
    center = values - jnp.mean(values, axis=-1, keepdims=True)
    inverse = lax.rsqrt(jnp.mean(center * center, axis=-1, keepdims=True) + EPSILON)
    return (center * inverse, inverse)


def norm_back(grad_normed, normed, inverse):
    mean_grad = jnp.mean(grad_normed, axis=-1, keepdims=True)
    mean_cross = jnp.mean(grad_normed * normed, axis=-1, keepdims=True)
    return inverse * (grad_normed - mean_grad - normed * mean_cross)


def matmul(left, right):
    return jnp.dot(left, right, preferred_element_type=jnp.float32)


def matmul_left_t(left, right):
    return lax.dot_general(
        left, right, (((0,), (0,)), ((), ())), preferred_element_type=jnp.float32
    )


def matmul_right_t(left, right):
    return lax.dot_general(
        left, right, (((1,), (1,)), ((), ())), preferred_element_type=jnp.float32
    )


def exact_gelu(values):
    return jax.nn.gelu(values, approximate=False)


def window_scores(packed, same_region, table_bias, head_dim):
    queries = packed[..., :head_dim]
    keys_all = packed[..., head_dim : 2 * head_dim]
    raw_scores = jnp.einsum(
        "wihd,wjhd->whij", queries, keys_all, preferred_element_type=jnp.float32
    )
    return jnp.where(
        same_region, raw_scores * (1.0 / math.sqrt(head_dim)) + table_bias[None], MASKED
    )


def attend(packed, same_region, table_bias, head_dim):
    masked = window_scores(packed, same_region, table_bias, head_dim)
    top_score = jnp.max(masked, axis=-1, keepdims=True)
    weights_exp = jnp.exp(masked - top_score)
    denominator = jnp.sum(weights_exp, axis=-1, keepdims=True)
    probabilities = (weights_exp / denominator).astype(jnp.bfloat16)
    attended = jnp.einsum(
        "whij,wjhd->wihd",
        probabilities,
        packed[..., 2 * head_dim :],
        preferred_element_type=jnp.float32,
    )
    return (attended.astype(jnp.bfloat16), top_score + jnp.log(denominator))


def attend_back(packed, same_region, table_bias, log_total, grad_attended, head_dim):
    masked = window_scores(packed, same_region, table_bias, head_dim)
    probabilities = jnp.exp(masked - log_total)
    grad_weights = jnp.einsum(
        "wihd,wjhd->whij",
        grad_attended,
        packed[..., 2 * head_dim :],
        preferred_element_type=jnp.float32,
    )
    inner = jnp.sum(probabilities * grad_weights, axis=-1, keepdims=True)
    grad_scores = (probabilities * (grad_weights - inner)).astype(jnp.bfloat16)
    score_scale = 1.0 / math.sqrt(head_dim)
    grad_queries = (
        jnp.einsum(
            "whij,wjhd->wihd",
            grad_scores,
            packed[..., head_dim : 2 * head_dim],
            preferred_element_type=jnp.float32,
        )
        * score_scale
    )
    grad_keys = (
        jnp.einsum(
            "whij,wihd->wjhd",
            grad_scores,
            packed[..., :head_dim],
            preferred_element_type=jnp.float32,
        )
        * score_scale
    )
    grad_values = jnp.einsum(
        "whij,wihd->wjhd",
        probabilities.astype(jnp.bfloat16),
        grad_attended,
        preferred_element_type=jnp.float32,
    )
    grad_packed = jnp.concatenate([grad_queries, grad_keys, grad_values], axis=-1).astype(
        jnp.bfloat16
    )
    return (grad_packed, jnp.sum(grad_scores, axis=0, dtype=jnp.float32))


def shards(
    inputs,
    norm0_gain,
    norm0_bias,
    merge_weight,
    norm1_gain,
    norm1_bias,
    qkv_weight,
    qkv_bias,
    rel_table,
    rel_index,
    regions,
    live_windows,
    proj_weight,
    proj_bias,
    norm2_gain,
    norm2_bias,
    up_weight,
    up_bias,
    down_weight,
    down_bias,
    cotangent,
):
    micro_count, strip_rows, in_width = inputs.shape
    model_width = merge_weight.shape[1]
    win_tokens = rel_index.shape[0]
    strip_windows = strip_rows // win_tokens
    strip_index = lax.axis_index("mp")
    qkv_full, qkv_bias_full, proj_full, up_full, up_bias_full, down_full, table_full = (
        lax.all_gather(qkv_weight, "mp", axis=1, tiled=True),
        lax.all_gather(qkv_bias, "mp", axis=0, tiled=True),
        lax.all_gather(proj_weight, "mp", axis=0, tiled=True),
        lax.all_gather(up_weight, "mp", axis=1, tiled=True),
        lax.all_gather(up_bias, "mp", axis=0, tiled=True),
        lax.all_gather(down_weight, "mp", axis=0, tiled=True),
        lax.all_gather(rel_table, "mp", axis=0, tiled=True),
    )
    head_count = qkv_full.shape[1]
    packed_width = qkv_full.shape[2]
    head_dim = proj_full.shape[1]
    hidden_width = up_full.shape[1]
    qkv_flat = qkv_full.reshape(model_width, head_count * packed_width)
    qkv_bias_flat = qkv_bias_full.reshape(head_count * packed_width).astype(jnp.float32)
    proj_flat = proj_full.reshape(model_width, model_width)
    up_bias_wide = up_bias_full.astype(jnp.float32)
    onehot_index = (rel_index[:, :, None] == jnp.arange(table_full.shape[1])[None, None, :]).astype(
        jnp.float32
    )
    table_heads = rel_table.astype(jnp.float32)
    table_bias = jnp.einsum("ijt,ht->hij", onehot_index, table_heads, precision=HIGHEST)
    window_in_group = strip_index * strip_windows + jnp.arange(strip_windows)
    live_window = (window_in_group[None, :] < live_windows[:, 0][:, None]).astype(jnp.float32)
    live_all = jnp.repeat(live_window, win_tokens, axis=1)
    grad_norm0_gain = jnp.zeros((in_width,), jnp.float32)
    grad_norm0_bias = jnp.zeros((in_width,), jnp.float32)
    grad_merge = jnp.zeros((in_width, model_width), jnp.float32)
    grad_norm1_gain = jnp.zeros((model_width,), jnp.float32)
    grad_norm1_bias = jnp.zeros((model_width,), jnp.float32)
    grad_qkv = jnp.zeros((model_width, head_count * packed_width), jnp.float32)
    grad_qkv_bias = jnp.zeros((head_count * packed_width,), jnp.float32)
    score_total = jnp.zeros((table_heads.shape[0], win_tokens, win_tokens), jnp.float32)
    grad_proj = jnp.zeros((model_width, model_width), jnp.float32)
    grad_proj_bias = jnp.zeros((model_width,), jnp.float32)
    grad_norm2_gain = jnp.zeros((model_width,), jnp.float32)
    grad_norm2_bias = jnp.zeros((model_width,), jnp.float32)
    grad_up = jnp.zeros((model_width, hidden_width), jnp.float32)
    grad_up_bias = jnp.zeros((hidden_width,), jnp.float32)
    grad_down = jnp.zeros((hidden_width, model_width), jnp.float32)
    grad_down_bias = jnp.zeros((model_width,), jnp.float32)
    outputs = []
    input_grads = []
    for micro_step in range(micro_count):
        live_rows = live_all[micro_step][:, None]
        values_in = inputs[micro_step].astype(jnp.float32)
        normed0, inverse0 = normalize(values_in)
        normed_in = (normed0 * norm0_gain + norm0_bias).astype(jnp.bfloat16)
        merged = matmul(normed_in, merge_weight)
        normed1, inverse1 = normalize(merged)
        normed_mid = (normed1 * norm1_gain + norm1_bias).astype(jnp.bfloat16)
        packed = (matmul(normed_mid, qkv_flat) + qkv_bias_flat).astype(jnp.bfloat16)
        packed = packed.reshape(strip_rows, head_count, packed_width)
        packed_heads = lax.all_to_all(packed, "mp", split_axis=1, concat_axis=0, tiled=True)
        group_rows = packed_heads.shape[0]
        region_rows = regions[micro_step]
        heads_here = packed_heads.shape[1]
        window_ids = region_rows.reshape(group_rows // win_tokens, win_tokens)
        same_region = window_ids[:, None, :, None] == window_ids[:, None, None, :]
        packed_windows = packed_heads.reshape(
            group_rows // win_tokens, win_tokens, heads_here, packed_width
        )
        attended_heads, log_total = attend(packed_windows, same_region, table_bias, head_dim)
        attended = lax.all_to_all(
            attended_heads.reshape(group_rows, heads_here, head_dim),
            "mp",
            split_axis=0,
            concat_axis=1,
            tiled=True,
        )
        attended = attended.reshape(strip_rows, model_width)
        middle = merged + matmul(attended, proj_flat) + proj_bias
        normed2, inverse2 = normalize(middle)
        normed_ffn = (normed2 * norm2_gain + norm2_bias).astype(jnp.bfloat16)
        pre_act = matmul(normed_ffn, up_full) + up_bias_wide
        activated = exact_gelu(pre_act).astype(jnp.bfloat16)
        outputs.append((middle + matmul(activated, down_full) + down_bias) * live_rows)
        grad_out = cotangent[micro_step].astype(jnp.float32) * live_rows
        grad_out_low = grad_out.astype(jnp.bfloat16)
        grad_down_bias = grad_down_bias + jnp.sum(grad_out, axis=0)
        grad_down = grad_down + matmul_left_t(activated, grad_out_low)
        grad_act = matmul_right_t(grad_out_low, down_full)
        gelu_value, gelu_pull = jax.vjp(exact_gelu, pre_act)
        grad_pre = gelu_pull(grad_act)[0].astype(jnp.bfloat16)
        grad_up_bias = grad_up_bias + jnp.sum(grad_pre, axis=0, dtype=jnp.float32)
        grad_up = grad_up + matmul_left_t(normed_ffn, grad_pre)
        grad_ffn = matmul_right_t(grad_pre, up_full)
        grad_norm2_gain = grad_norm2_gain + jnp.sum(grad_ffn * normed2, axis=0)
        grad_norm2_bias = grad_norm2_bias + jnp.sum(grad_ffn, axis=0)
        grad_middle = grad_out + norm_back(grad_ffn * norm2_gain, normed2, inverse2)
        grad_attn = grad_middle.astype(jnp.bfloat16)
        grad_proj_bias = grad_proj_bias + jnp.sum(grad_attn, axis=0, dtype=jnp.float32)
        grad_proj = grad_proj + matmul_left_t(attended, grad_attn)
        grad_attended = matmul_right_t(grad_attn, proj_flat).astype(jnp.bfloat16)
        grad_attended = grad_attended.reshape(strip_rows, head_count, head_dim)
        grad_heads = lax.all_to_all(grad_attended, "mp", split_axis=1, concat_axis=0, tiled=True)
        grad_windows = grad_heads.reshape(
            group_rows // win_tokens, win_tokens, heads_here, head_dim
        )
        grad_packed, score_part = attend_back(
            packed_windows, same_region, table_bias, log_total, grad_windows, head_dim
        )
        score_total = score_total + score_part
        grad_packed = grad_packed.reshape(group_rows, heads_here, packed_width)
        grad_packed = lax.all_to_all(grad_packed, "mp", split_axis=0, concat_axis=1, tiled=True)
        grad_flat = grad_packed.reshape(strip_rows, head_count * packed_width)
        grad_qkv_bias = grad_qkv_bias + jnp.sum(grad_flat, axis=0, dtype=jnp.float32)
        grad_qkv = grad_qkv + matmul_left_t(normed_mid, grad_flat)
        grad_mid = matmul_right_t(grad_flat, qkv_flat)
        grad_norm1_gain = grad_norm1_gain + jnp.sum(grad_mid * normed1, axis=0)
        grad_norm1_bias = grad_norm1_bias + jnp.sum(grad_mid, axis=0)
        grad_merged = (grad_middle + norm_back(grad_mid * norm1_gain, normed1, inverse1)).astype(
            jnp.bfloat16
        )
        grad_merge = grad_merge + matmul_left_t(normed_in, grad_merged)
        grad_low = matmul_right_t(grad_merged, merge_weight)
        grad_norm0_gain = grad_norm0_gain + jnp.sum(grad_low * normed0, axis=0)
        grad_norm0_bias = grad_norm0_bias + jnp.sum(grad_low, axis=0)
        input_grads.append(norm_back(grad_low * norm0_gain, normed0, inverse0))
    table_grad = jnp.einsum("hij,ijt->ht", score_total, onehot_index, precision=HIGHEST)
    qkv_whole = grad_qkv.reshape(model_width, head_count, packed_width)
    qkv_bias_whole = grad_qkv_bias.reshape(head_count, packed_width)
    proj_whole = grad_proj.reshape(head_count, head_dim, model_width)
    qkv_part, qkv_bias_part, proj_part, up_part, up_bias_part, down_part = (
        lax.psum_scatter(
            qkv_whole.astype(jnp.bfloat16), "mp", scatter_dimension=1, tiled=True
        ).astype(jnp.float32),
        lax.psum_scatter(
            qkv_bias_whole.astype(jnp.bfloat16), "mp", scatter_dimension=0, tiled=True
        ).astype(jnp.float32),
        lax.psum_scatter(
            proj_whole.astype(jnp.bfloat16), "mp", scatter_dimension=0, tiled=True
        ).astype(jnp.float32),
        lax.psum_scatter(
            grad_up.astype(jnp.bfloat16), "mp", scatter_dimension=1, tiled=True
        ).astype(jnp.float32),
        lax.psum_scatter(
            grad_up_bias.astype(jnp.bfloat16), "mp", scatter_dimension=0, tiled=True
        ).astype(jnp.float32),
        lax.psum_scatter(
            grad_down.astype(jnp.bfloat16), "mp", scatter_dimension=0, tiled=True
        ).astype(jnp.float32),
    )
    qkv_sum, qkv_bias_sum, proj_sum, up_sum, up_bias_sum, down_sum, table_sum = (
        lax.psum(qkv_part.astype(jnp.bfloat16), "dp").astype(jnp.float32),
        lax.psum(qkv_bias_part.astype(jnp.bfloat16), "dp").astype(jnp.float32),
        lax.psum(proj_part.astype(jnp.bfloat16), "dp").astype(jnp.float32),
        lax.psum(up_part.astype(jnp.bfloat16), "dp").astype(jnp.float32),
        lax.psum(up_bias_part.astype(jnp.bfloat16), "dp").astype(jnp.float32),
        lax.psum(down_part.astype(jnp.bfloat16), "dp").astype(jnp.float32),
        lax.psum(table_grad.astype(jnp.bfloat16), "dp").astype(jnp.float32),
    )
    (
        merge_sum,
        gain0_sum,
        bias0_sum,
        gain1_sum,
        bias1_sum,
        gain2_sum,
        bias2_sum,
        proj_bias_sum,
        down_bias_sum,
    ) = lax.psum(
        (
            grad_merge,
            grad_norm0_gain,
            grad_norm0_bias,
            grad_norm1_gain,
            grad_norm1_bias,
            grad_norm2_gain,
            grad_norm2_bias,
            grad_proj_bias,
            grad_down_bias,
        ),
        ("dp", "mp"),
    )
    return (
        jnp.stack(outputs),
        jnp.stack(input_grads),
        gain0_sum,
        bias0_sum,
        merge_sum,
        gain1_sum,
        bias1_sum,
        qkv_sum,
        qkv_bias_sum,
        table_sum,
        proj_sum,
        proj_bias_sum,
        gain2_sum,
        bias2_sum,
        up_sum,
        up_bias_sum,
        down_sum,
        down_bias_sum,
    )


def solution(mesh):
    placed = (
        P(None, ("dp", "mp"), None),
        P(),
        P(),
        P(),
        P(),
        P(),
        P(None, "mp", None),
        P("mp", None),
        P("mp", None),
        P(),
        P(None, "dp"),
        P(None, "dp"),
        P("mp", None, None),
        P(),
        P(),
        P(),
        P(None, "mp"),
        P("mp"),
        P("mp", None),
        P(),
        P(None, ("dp", "mp"), None),
    )
    return jax.shard_map(
        shards,
        mesh=mesh,
        in_specs=placed,
        out_specs=(
            P(None, ("dp", "mp"), None),
            P(None, ("dp", "mp"), None),
            P(),
            P(),
            P(),
            P(),
            P(),
            P(None, "mp", None),
            P("mp", None),
            P("mp", None),
            P("mp", None, None),
            P(),
            P(),
            P(),
            P(None, "mp"),
            P("mp"),
            P("mp", None),
            P(),
        ),
        check_vma=False,
    )
```

profile of v0, /device:TPU:0, one launch (start us, length us, event | category | flops | bytes accessed | tf_op | source)
XLA Modules:
  0.0 1139.3 jit_solution(18316722843151651680)
XLA Ops:
  27.3 11.1 all-gather.6.cloned.1.call-done
  70.3 38.6 %all-to-all-done.2 = bf16[1176,16,96]{0,2,1:T(8,128)(2,1)} async-done(((bf16[1176,16,96]{0,2,1:T(8,128)(2,1)}), bf16[1176,16,96]{0,2,1:T(8,128)(2,1)}, u32[]{:S(2)}, u32[]{:S(2)}) %all-to-all-start.2) | async-done | bytes 3612704 | tf_op jit(solution)/shard_map/all_to_all | solution.py:194
  114.3 56.9 %all-gather.1 = bf16[8,1,256]{2,1,0:T(2,128)(2,1)S(1)} all-gather(bf16[1,1,256]{2,1,0:T(2,128)(2,1)S(1)} %reshape.338), channel_id=1, replica_groups=mesh['dp'=4,'mp'=8] {'mp'}, dimensions={0}, use_global_device_ids=true | all-gather | bytes 4608 | tf_op jit(solution)/shard_map/all_gather | solution.py:146
  200.7 11.6 %copy.100 = bf16[1176,8,2,96]{3,2,0,1:T(2,128)(2,1)} copy(bf16[1176,8,2,96]{0,3,2,1:T(8,128)(2,1)} %bitcast.22) | data formatting | bytes 7225344 | tf_op jit(solution)/shard_map/all_to_all | solution.py:194
  212.3 11.6 %copy.90 = bf16[1176,8,2,96]{3,2,0,1:T(2,128)(2,1)} copy(bf16[1176,8,2,96]{0,3,2,1:T(8,128)(2,1)} %bitcast.4) | data formatting | bytes 7225344 | tf_op jit(solution)/shard_map/all_to_all | solution.py:194
  224.0 17.2 %fusion.117 = (bf16[192,49,2,32]{3,2,1,0:T(2,128)(2,1)}, bf16[192,49,2,32]{3,2,1,0:T(2,128)(2,1)}, bf16[192,49,2,32]{3,2,1,0:T(2,128)(2,1)}) fusion(bf16[192,49,2,96]{3,2,1,0:T(2,128)(2,1)} %bitcast.272), kind=kLoop, calls=%fused_computation.240 | loop fusion | bytes 7225344 | tf_op jit(solution)/shard_map/slice | solution.py:47
  241.1 11.1 copy.148
  252.2 11.0 copy.147
  263.2 11.1 copy.146
  274.3 17.1 %fusion.118 = (bf16[192,49,2,32]{3,2,1,0:T(2,128)(2,1)}, bf16[192,49,2,32]{3,2,1,0:T(2,128)(2,1)}, bf16[192,49,2,32]{3,2,1,0:T(2,128)(2,1)}) fusion(bf16[192,49,2,96]{3,2,1,0:T(2,128)(2,1)} %bitcast.271), kind=kLoop, calls=%fused_computation.241 | loop fusion | bytes 7225344 | tf_op jit(solution)/shard_map/slice | solution.py:47
  291.4 11.0 copy.151
  302.4 11.1 copy.150
  313.5 11.4 %copy.149 = bf16[192,49,2,32]{1,3,2,0:T(8,128)(2,1)} copy(bf16[192,49,2,32]{3,2,1,0:T(2,128)(2,1)} %get-tuple-element.88) | data formatting | bytes 2408448
  341.9 11.3 copy.143
  382.9 11.3 copy.142
  453.1 27.0 %multiply_convert_fusion.3 = (bf16[1176,2048]{1,0:T(8,128)(2,1)}, f32[1176,2048]{1,0:T(8,128)}, f32[1176,2048]{1,0:T(8,128)}) fusion(f32[2048]{0:T(1024)S(1)} %bitcast.308, bf16[512,2048]{1,0:T(8,128)(2,1)} %all-gather.8.cloned.1.call-done, f32[1176,512]{1,0:T(8,128)S(1)} %get-tuple-element.112, f32[512]{0:T(512)S(1)} %copy-done.51, f32[512]{0:T(512)S(1)} %copy-done.45, ...), kind=kOutput, calls=%fused_computation.38 | convolution fusion | flops 2628218880 | bytes 28611776 | tf_op jit(solution)/shard_map/dot_general | solution.py:26
  480.1 10.9 convert_reduce_fusion.3
  496.1 26.0 %multiply_convert_fusion.2 = (bf16[1176,2048]{1,0:T(8,128)(2,1)}, f32[1176,2048]{1,0:T(8,128)}, f32[1176,2048]{1,0:T(8,128)}) fusion(f32[2048]{0:T(1024)S(1)} %bitcast.309, bf16[512,2048]{1,0:T(8,128)(2,1)S(1)} %copy-done.82, f32[1176,512]{1,0:T(8,128)S(1)} %copy-done.6, f32[1176]{0:T(1024)S(1)} %add_rsqrt_fusion, f32[1176]{0:T(1024)S(1)} %broadcast_multiply_fusion.8, ...), kind=kOutput, calls=%fused_computation.25 | convolution fusion | flops 2628218880 | bytes 28611776 | tf_op jit(solution)/shard_map/dot_general | solution.py:26
  620.5 16.2 %multiply_reduce_fusion = (f32[192,2,49]{2,1,0:T(2,128)}, f32[192,2,49,49]{2,3,1,0:T(8,128)}) fusion(f32[192,2,49,49]{2,3,1,0:T(8,128)} %copy-done.1, f32[192,2,49]{2,1,0:T(2,128)S(1)} %bitcast.298, bf16[192,49,2,32]{1,3,2,0:T(8,128)(2,1)} %copy.149, bf16[192,49,2,32]{1,0,3,2:T(8,128)(2,1)S(1)} %copy-done.10), kind=kOutput, calls=%fused_computation.5 | convolution fusion | flops 61754112 | bytes 9934848 | tf_op jit(solution)/shard_map/wihd,wjhd->whij/dot_general | solution.py:74
  645.8 11.0 convert_bitcast_fusion.3
  656.8 15.9 %multiply_reduce_fusion.1 = (f32[192,2,49]{2,1,0:T(2,128)S(1)}, f32[192,2,49,49]{2,3,1,0:T(8,128)}) fusion(f32[192,2,49,49]{2,3,1,0:T(8,128)} %copy-done.2, f32[192,2,49]{2,1,0:T(2,128)S(1)} %bitcast.300, bf16[192,49,2,32]{1,3,2,0:T(8,128)(2,1)} %copy.146, bf16[192,49,2,32]{1,0,3,2:T(8,128)(2,1)S(1)} %copy-done.11), kind=kOutput, calls=%fused_computation.8 | convolution fusion | flops 61754112 | bytes 9934848 | tf_op jit(solution)/shard_map/wihd,wjhd->whij/dot_general | solution.py:74
  737.2 11.1 copy.118
  793.8 11.0 copy.130
  828.3 11.6 %copy.119 = bf16[8,1176,2,96]{1,3,2,0:T(8,128)(2,1)} copy(bf16[8,1176,2,96]{3,2,1,0:T(2,128)(2,1)} %bitcast.40) | data formatting | bytes 7225344 | tf_op jit(solution)/shard_map/all_to_all | solution.py:245
  850.7 18.4 %all-to-all-done.7 = bf16[9408,2,96]{2,1,0:T(2,128)(2,1)} async-done(((bf16[9408,2,96]{2,1,0:T(2,128)(2,1)}), bf16[9408,2,96]{2,1,0:T(2,128)(2,1)}, u32[]{:S(2)}, u32[]{:S(2)}) %all-to-all-start.7) | async-done | bytes 3612704 | tf_op jit(solution)/shard_map/all_to_all | solution.py:245
  869.1 11.6 %copy.131 = bf16[8,1176,2,96]{1,3,2,0:T(8,128)(2,1)} copy(bf16[8,1176,2,96]{3,2,1,0:T(2,128)(2,1)} %bitcast.51) | data formatting | bytes 7225344 | tf_op jit(solution)/shard_map/all_to_all | solution.py:245
  918.7 22.8 %reduce-scatter.5.cloned.1.call-done = bf16[512,2,96]{0,2,1:T(8,128)(2,1)} async-done(((bf16[512,16,96]{0,2,1:T(8,128)(2,1)}), bf16[512,2,96]{0,2,1:T(8,128)(2,1)}) %reduce-scatter.5.cloned.1.call-update) | async-done | bytes 196624 | tf_op jit(solution)/shard_map/reduce_scatter | solution.py:265
  947.5 11.2 fusion.38
  959.4 13.4 %all-reduce.3 = (bf16[16,96]{1,0:T(8,128)(2,1)S(1)}, bf16[2048]{0:T(1024)(128)(2,1)S(1)}) all-reduce(bf16[16,96]{1,0:T(8,128)(2,1)S(1)} %bitcast.307, bf16[2048]{0:T(1024)(128)(2,1)S(1)} %add_convert_fusion.10), channel_id=3, replica_groups=mesh['dp'=4,'mp'=8] {'mp'}, use_global_device_ids=true, to_apply=%region_47.48.clone | all-reduce | flops 3584 | bytes 14336
  972.9 11.5 %all-reduce.4 = (bf16[2,96]{1,0:T(2,128)(2,1)S(1)}, bf16[2,169]{1,0:T(2,128)(2,1)S(1)}, bf16[256]{0:T(256)(128)(2,1)S(1)}) all-reduce(bf16[2,96]{1,0:T(2,128)(2,1)S(1)} %constant_dynamic-slice_fusion, bf16[2,169]{1,0:T(2,128)(2,1)S(1)} %copy-done.79, bf16[256]{0:T(256)(128)(2,1)S(1)} %dynamic-slice.3), channel_id=1, replica_groups=mesh['dp'=4,'mp'=8] {'dp'}, use_global_device_ids=true, to_apply=%region_48.49 | all-reduce | flops 786 | bytes 3144 | tf_op jit(solution)/shard_map/psum | solution.py:286
  986.1 37.7 %all-reduce.2 = (f32[1024]{0:T(1024)}, f32[1024]{0:T(1024)}, f32[512]{0:T(512)}, f32[512]{0:T(512)}, f32[512]{0:T(512)}, /*index=5*/f32[512]{0:T(512)}, f32[512]{0:T(512)}, f32[512]{0:T(512)}) all-reduce(f32[1024]{0:T(1024)S(1)} %add.354, f32[1024]{0:T(1024)S(1)} %add.355, ...), channel_id=1, replica_groups=mesh['dp'=4,'mp'=8] {'dp','mp'}, use_global_device_ids=true, to_apply=%region_32.33 | all-reduce | flops 5120 | bytes 40960 | tf_op jit(solution)/shard_map/psum | solution.py:303
  1040.3 89.0 %all-reduce.9.cloned.1.call-done = f32[1024,512]{1,0:T(8,128)} async-done(((f32[1024,512]{1,0:T(8,128)}), f32[1024,512]{1,0:T(8,128)}) %all-reduce.9.cloned.1.call-update) | async-done | bytes 2097168 | tf_op jit(solution)/shard_map/psum | solution.py:303
  (377 shorter events, 512.9 us)
Async XLA Ops:
  7.2 17.3 %copy-start = (bf16[1024,512]{1,0:T(8,128)(2,1)S(1)}, bf16[1024,512]{1,0:T(8,128)(2,1)}, u32[]{:S(2)}) copy-start(bf16[1024,512]{1,0:T(8,128)(2,1)} %param.24) | copy-start | bytes 3145732
  7.2 31.1 %all-gather.6.cloned.1.call-start = ((), (), s32[]{:S(2)}) async-start(), calls=%async_computation.12 | async-start | bytes 1769472 | tf_op jit(solution)/shard_map/all_gather | solution.py:142
  21.7 33.2 %copy-start.43 = (f32[1176]{0:T(1024)}, f32[1176]{0:T(1024)S(1)}, u32[]{:S(2)}) copy-start(f32[1176]{0:T(1024)S(1)} %broadcast_multiply_fusion.17) | copy-start | bytes 14116
  26.7 399.2 %copy-start.12 = (f32[1176,512]{1,0:T(8,128)}, f32[1176,512]{1,0:T(8,128)S(1)}, u32[]{:S(2)}) copy-start(f32[1176,512]{1,0:T(8,128)S(1)} %get-tuple-element.101) | copy-start | bytes 7225348
  26.7 17.0 %copy-start.52 = (f32[1176]{0:T(1024)}, f32[1176]{0:T(1024)S(1)}, u32[]{:S(2)}) copy-start(f32[1176]{0:T(1024)S(1)} %broadcast_multiply_fusion.9) | copy-start | bytes 14116
  27.3 16.5 %copy-start.61 = (f32[1176]{0:T(1024)}, f32[1176]{0:T(1024)S(1)}, u32[]{:S(2)}) copy-start(f32[1176]{0:T(1024)S(1)} %add_rsqrt_fusion.1) | copy-start | bytes 14116
  49.7 59.2 %all-to-all-start.2 = ((bf16[1176,16,96]{0,2,1:T(8,128)(2,1)}), bf16[1176,16,96]{0,2,1:T(8,128)(2,1)}, u32[]{:S(2)}, u32[]{:S(2)}) async-start(bf16[1176,16,96]{0,2,1:T(8,128)(2,1)} %bitcast.282), calls=%async_computation.2 | async-start | bytes 7864320 | tf_op jit(solution)/shard_map/all_to_all | solution.py:194
  54.2 398.8 %all-gather.8.cloned.1.call-start = ((), (), s32[]{:S(2)}) async-start(), calls=%async_computation.13 | async-start | bytes 2359296 | tf_op jit(solution)/shard_map/all_gather | solution.py:145
  108.9 63.0 %copy-start.80 = (s32[2,1]{0,1:T(1,128)S(1)}, s32[2,1]{0,1:T(1,128)}, u32[]{:S(2)}) copy-start(s32[2,1]{0,1:T(1,128)} %param.32) | copy-start | bytes 28
  108.9 64.6 %copy-start.90 = (bf16[2,169]{1,0:T(2,128)(2,1)S(1)}, bf16[2,169]{1,0:T(2,128)(2,1)}, u32[]{:S(2)}) copy-start(bf16[2,169]{1,0:T(2,128)(2,1)} %param.29) | copy-start | bytes 2032
  108.9 68.2 %copy-start.46 = (s32[2,9408]{1,0:T(2,128)S(1)}, s32[2,9408]{1,0:T(2,128)}, u32[]{:S(2)}) copy-start(s32[2,9408]{1,0:T(2,128)} %param.31) | copy-start | bytes 225796
  108.9 103.4 %all-to-all-start = ((bf16[1176,16,96]{0,2,1:T(8,128)(2,1)}), bf16[1176,16,96]{0,2,1:T(8,128)(2,1)}, u32[]{:S(2)}, u32[]{:S(2)}) async-start(bf16[1176,16,96]{0,2,1:T(8,128)(2,1)} %bitcast.279), calls=%async_computation | async-start | bytes 7864320 | tf_op jit(solution)/shard_map/all_to_all | solution.py:194
  113.6 366.5 %all-gather.10.cloned.1.call-start = ((), (), s32[]{:S(2)}) async-start(), calls=%async_computation.14 | async-start | bytes 2359296 | tf_op jit(solution)/shard_map/all_gather | solution.py:147
  361.5 40.9 %all-to-all-start.3 = ((bf16[8,2,37632]{2,1,0:T(2,128)(2,1)}), bf16[8,2,37632]{2,1,0:T(2,128)(2,1)}, u32[]{:S(2)}, u32[]{:S(2)}) async-start(bf16[8,2,37632]{2,1,0:T(2,128)(2,1)} %reshape.349), calls=%async_computation.3 | async-start | bytes 2408448 | tf_op jit(solution)/shard_map/all_to_all | solution.py:204
  402.4 27.8 %all-to-all-start.1 = ((bf16[8,2,37632]{2,1,0:T(2,128)(2,1)}), bf16[8,2,37632]{2,1,0:T(2,128)(2,1)}, u32[]{:S(2)}, u32[]{:S(2)}) async-start(bf16[8,2,37632]{2,1,0:T(2,128)(2,1)} %reshape.351), calls=%async_computation.1 | async-start | bytes 2408448 | tf_op jit(solution)/shard_map/all_to_all | solution.py:204
  406.7 512.0 %reduce-scatter.7.cloned.1.call-start = ((), (), s32[]{:S(2)}) async-start(), calls=%async_computation.17 | async-start | bytes 589824 | tf_op jit(solution)/shard_map/reduce_scatter | solution.py:271
  453.0 27.0 %copy-start.60 = (f32[1176]{0:T(1024)S(1)}, f32[1176]{0:T(1024)}, u32[]{:S(2)}) copy-start(f32[1176]{0:T(1024)} %broadcast_in_dim.37) | copy-start | bytes 14116
  496.1 26.0 %copy-start.35 = (bf16[2,1176,512]{2,1,0:T(8,128)(2,1)S(1)}, bf16[2,1176,512]{2,1,0:T(8,128)(2,1)}, u32[]{:S(2)}) copy-start(bf16[2,1176,512]{2,1,0:T(8,128)(2,1)} %param.41) | copy-start | bytes 7225348
  496.1 26.0 %copy-start.59 = (f32[1176]{0:T(1024)S(1)}, f32[1176]{0:T(1024)}, u32[]{:S(2)}) copy-start(f32[1176]{0:T(1024)} %broadcast_in_dim.40) | copy-start | bytes 14116
  551.3 367.5 %reduce-scatter.9.cloned.1.call-start = ((), (), s32[]{:S(2)}) async-start(), calls=%async_computation.18 | async-start | bytes 2359296 | tf_op jit(solution)/shard_map/reduce_scatter | solution.py:274
  571.6 24.9 %all-to-all-start.6 = ((bf16[1176,16,32]{0,2,1:T(8,128)(2,1)}), bf16[1176,16,32]{0,2,1:T(8,128)(2,1)}, u32[]{:S(2)}, u32[]{:S(2)}) async-start(bf16[1176,16,32]{0,2,1:T(8,128)(2,1)} %bitcast.293), calls=%async_computation.6 | async-start | bytes 2621440 | tf_op jit(solution)/shard_map/all_to_all | solution.py:236
  575.9 342.8 %reduce-scatter.11.cloned.1.call-start = ((), (), s32[]{:S(2)}) async-start(), calls=%async_computation.19 | async-start | bytes 2359296 | tf_op jit(solution)/shard_map/reduce_scatter | solution.py:280
  596.6 40.1 %all-to-all-start.4 = ((bf16[1176,16,32]{0,2,1:T(8,128)(2,1)}), bf16[1176,16,32]{0,2,1:T(8,128)(2,1)}, u32[]{:S(2)}, u32[]{:S(2)}) async-start(bf16[1176,16,32]{0,2,1:T(8,128)(2,1)} %bitcast.292), calls=%async_computation.4 | async-start | bytes 2621440 | tf_op jit(solution)/shard_map/all_to_all | solution.py:236
  748.3 60.4 %all-to-all-start.5 = ((bf16[9408,2,96]{2,1,0:T(2,128)(2,1)}), bf16[9408,2,96]{2,1,0:T(2,128)(2,1)}, u32[]{:S(2)}, u32[]{:S(2)}) async-start(bf16[9408,2,96]{2,1,0:T(2,128)(2,1)} %copy.118), calls=%async_computation.5 | async-start | bytes 9633792 | tf_op jit(solution)/shard_map/all_to_all | solution.py:245
  808.7 60.4 %all-to-all-start.7 = ((bf16[9408,2,96]{2,1,0:T(2,128)(2,1)}), bf16[9408,2,96]{2,1,0:T(2,128)(2,1)}, u32[]{:S(2)}, u32[]{:S(2)}) async-start(bf16[9408,2,96]{2,1,0:T(2,128)(2,1)} %copy.130), calls=%async_computation.7 | async-start | bytes 9633792 | tf_op jit(solution)/shard_map/all_to_all | solution.py:245
  813.3 128.2 %reduce-scatter.5.cloned.1.call-start = ((), (), s32[]{:S(2)}) async-start(), calls=%async_computation.16 | async-start | bytes 1769472 | tf_op jit(solution)/shard_map/reduce_scatter | solution.py:265
  903.8 129.7 %all-reduce.11.cloned.1.call-start = ((), (), s32[]{:S(2)}) async-start(), calls=%async_computation.20 | async-start | bytes 1572864 | tf_op jit(solution)/shard_map/psum | solution.py:285
  915.8 25.8 %copy-start.37 = (bf16[1176,512]{1,0:T(8,128)(2,1)S(1)}, bf16[1176,512]{1,0:T(8,128)(2,1)}, u32[]{:S(2)}) copy-start(bf16[1176,512]{1,0:T(8,128)(2,1)} %copy-done.36) | copy-start | bytes 3612676
  915.8 25.8 %copy-start.72 = (f32[1024]{0:T(1024)S(1)}, f32[1024]{0:T(1024)}, u32[]{:S(2)}) copy-start(f32[1024]{0:T(1024)} %param.23) | copy-start | bytes 12292
  941.5 187.8 %all-reduce.9.cloned.1.call-start = ((), (), s32[]{:S(2)}) async-start(), calls=%async_computation.15 | async-start | bytes 4194304 | tf_op jit(solution)/shard_map/psum | solution.py:303
  958.7 27.3 %copy-start.76 = (f32[512]{0:T(512)S(1)}, f32[512]{0:T(512)}, u32[]{:S(2)}) copy-start(f32[512]{0:T(512)} %get-tuple-element.48) | copy-start | bytes 6148
  958.7 27.3 %copy-start.75 = (f32[512]{0:T(512)S(1)}, f32[512]{0:T(512)}, u32[]{:S(2)}) copy-start(f32[512]{0:T(512)} %get-tuple-element.26) | copy-start | bytes 6148
  (80 other events, 499.2 us)
Sparse Core Ops, SparseCore 0:
  9.9 28.3 all-gather.5
  56.9 47.4 all-gather.7
  116.3 47.3 all-gather.9
  551.4 38.1 reduce-scatter.6
  593.0 43.2 reduce-scatter.8
  639.5 41.2 reduce-scatter.10
  903.9 37.5 reduce-scatter.4
  944.3 44.8 all-reduce.10
  996.0 133.2 all-reduce.8
where the time goes:
time: 1160 us; the launch traced here: 1140 us
  local copies, waits for them, and re-layouts  367 us (32%)
  matrix products  298 us (26%)
  waiting for transfers between devices  186 us (16%)
  blocking collectives  140 us (12%)
  other arithmetic  95.6 us (8%)
  starting transfers between devices  36.2 us (3%)
  between operations  16.8 us (1%)
    unnamed x205, local copies, waits for them, and re-layouts  113 us
    psum x1, waiting for transfers between devices, shards(): lax.psum((grad_merge, grad_norm0_gain, grad_norm0_bias, grad_norm1_gain,...  89 us
    dot_general x10, matrix products, matmul(): return jnp.dot(left, right, preferred_element_type=jnp.float32)  81.8 us
    dot_general x10, matrix products, matmul_right_t(): lax.dot_general(left, right, (((1,), (1,)), ((), ())), preferred_element_...  64.7 us
    concatenate x8, local copies, waits for them, and re-layouts, attend_back(): jnp.concatenate([grad_queries, grad_keys, grad_values], axis=-1)  57.7 us
    all_gather x1, blocking collectives, shards(): lax.all_gather(up_bias, 'mp', axis=0, tiled=True)  56.9 us
    dot_general x10, matrix products, matmul_left_t(): lax.dot_general(left, right, (((0,), (0,)), ((), ())), preferred_element_...  55 us
    all_to_all x2, waiting for transfers between devices, shards(): lax.all_to_all(packed, 'mp', split_axis=1, concat_axis=0, tiled=True)  38.6 us
  transfers between devices with their start and end apart: 17, of which 6 were waited for; matrix products, arithmetic and copies ran while one was open for 59% of the time, Pallas kernels for 0%

commit v1 on v0

v1 whole, which is shorter than its diff:
```python
import functools
import math

import jax
import jax.numpy as jnp
from jax import lax
from jax.experimental import pallas as pl
from jax.experimental.pallas import tpu as pltpu
from jax.sharding import PartitionSpec as P

F32 = jnp.float32
BF16 = jnp.bfloat16
EPSILON = 1e-05
MASKED = -1e30
COVER = 64
TILE = 16
GROUP = 4
VMEM_LIMIT = 60 << 20


def dot(left, right):
    return jnp.dot(left, right, preferred_element_type=F32)


def dot_rt(left, right):
    return lax.dot_general(left, right, (((1,), (1,)), ((), ())), preferred_element_type=F32)


def dot_lt(left, right):
    return lax.dot_general(left, right, (((0,), (0,)), ((), ())), preferred_element_type=F32)


def whole(shape):
    return pl.BlockSpec(shape, lambda i: (0,) * len(shape), pipeline_mode=pl.Buffered(1))


def call(kernel, grid, ins, in_specs, outs, out_specs, scratch, flops, nbytes):
    return pl.pallas_call(
        kernel,
        grid=(grid,),
        in_specs=in_specs,
        out_specs=out_specs,
        out_shape=outs,
        scratch_shapes=scratch,
        compiler_params=pltpu.CompilerParams(
            dimension_semantics=("arbitrary",), vmem_limit_bytes=VMEM_LIMIT
        ),
        cost_estimate=pl.CostEstimate(flops=flops, bytes_accessed=nbytes, transcendentals=0),
    )(*ins)


def spans(total, step):
    return [(start, min(step, total - start)) for start in range(0, total, step)]


def norm_parts(values):
    center = values - jnp.mean(values, axis=-1, keepdims=True)
    inverse = lax.rsqrt(jnp.mean(center * center, axis=-1, keepdims=True) + EPSILON)
    return center * inverse, inverse


def norm_back(grad, normed, inverse):
    mean_grad = jnp.mean(grad, axis=-1, keepdims=True)
    mean_cross = jnp.mean(grad * normed, axis=-1, keepdims=True)
    return inverse * (grad - mean_grad - normed * mean_cross)


def head_mask(head_dim):
    rows = lax.broadcasted_iota(jnp.int32, (GROUP * COVER, GROUP * head_dim), 0) // COVER
    cols = lax.broadcasted_iota(jnp.int32, (GROUP * COVER, GROUP * head_dim), 1) // head_dim
    return (rows == cols).astype(F32).astype(BF16)


def tiled(block, mask):
    return jnp.concatenate([block] * GROUP, axis=0) * mask


def merge_kernel(x_ref, g0_ref, b0_ref, wm_ref, g1_ref, b1_ref, merged_ref, mid_ref):
    normed, _ = norm_parts(x_ref[...].astype(F32))
    normed_in = (normed * g0_ref[...] + b0_ref[...]).astype(BF16)
    merged = dot(normed_in, wm_ref[...])
    merged_ref[...] = merged
    normed1, _ = norm_parts(merged)
    mid_ref[...] = (normed1 * g1_ref[...] + b1_ref[...]).astype(BF16)


def merge_rows(x, g0, b0, wm, g1, b1):
    rows, wide = x.shape
    width = wm.shape[1]
    step = rows // 7
    return call(
        merge_kernel,
        7,
        (x, g0, b0, wm, g1, b1),
        [
            pl.BlockSpec((step, wide), lambda i: (i, 0)),
            whole((1, wide)),
            whole((1, wide)),
            whole((wide, width)),
            whole((1, width)),
            whole((1, width)),
        ],
        [
            jax.ShapeDtypeStruct((rows, width), F32),
            jax.ShapeDtypeStruct((rows, width), BF16),
        ],
        [
            pl.BlockSpec((step, width), lambda i: (i, 0)),
            pl.BlockSpec((step, width), lambda i: (i, 0)),
        ],
        [],
        2 * rows * wide * width,
        rows * (2 * wide + 6 * width),
    )


def index_onehot(row, table_width):
    entry = lax.broadcasted_iota(jnp.int32, (table_width, row.shape[1]), 0)
    return (entry == row).astype(F32).astype(BF16)


def attn_kernel(
    head_dim,
    mid_ref,
    w_ref,
    qb_ref,
    tab_ref,
    idx_ref,
    ridc_ref,
    ridr_ref,
    q_ref,
    k_ref,
    v_ref,
    att_ref,
    rinv_ref,
    p_ref,
    wt_s,
    base_s,
    bias_s,
    mask_s,
):
    step = pl.program_id(0)
    rows, width = mid_ref.shape
    heads = width // head_dim
    lanes = GROUP * head_dim
    groups = heads // GROUP
    scale = 1.0 / math.sqrt(head_dim)
    outs = (q_ref, k_ref, v_ref)

    @pl.when(step == 0)
    def _():
        mask_s[...] = head_mask(head_dim)
        att_ref[...] = jnp.zeros_like(att_ref)
        rinv_ref[...] = jnp.zeros_like(rinv_ref)
        shards, local = w_ref.shape[0], w_ref.shape[1] // (3 * head_dim)
        for s in range(shards):
            for l in range(local):
                for t in range(3):
                    at = t * width + (s * local + l) * head_dim
                    wt_s[at : at + head_dim, :] = w_ref[
                        s, (3 * l + t) * head_dim : (3 * l + t + 1) * head_dim, :
                    ]
        part = rows // 7

        def project(i, _):
            here = pl.ds(pl.multiple_of(i * part, TILE), part)
            x = mid_ref[here, :]
            for t in range(3):
                y = dot_rt(x, wt_s[t * width : (t + 1) * width, :])
                y = y + qb_ref[:, t * width : (t + 1) * width]
                if t == 0:
                    y = y * scale
                outs[t][here, :] = y.astype(BF16)
            return 0

        lax.fori_loop(0, 7, project, 0)
        base_s[...] = jnp.full(base_s.shape, MASKED, F32)
        table = tab_ref[...]
        for pair in range(idx_ref.shape[0]):
            row = idx_ref[pair : pair + 1, :]
            vals = dot(table, index_onehot(row, table.shape[1]))
            vals = jnp.where(row < 0, MASKED, vals)
            base_s[:, 2 * pair, :] = vals[:, :COVER]
            base_s[:, 2 * pair + 1, :] = vals[:, COVER:]
        for g in range(groups):
            full = jnp.concatenate([base_s[g * GROUP + h] for h in range(GROUP)], axis=1)

            def shift(o, _):
                bias_s[o, g] = pltpu.roll(pltpu.roll(full, o, 0), o, 1)
                return 0

            lax.fori_loop(0, TILE, shift, 0)

    low_half = lax.broadcasted_iota(jnp.int32, (COVER, 2 * COVER), 1) < COVER
    sets = ridc_ref.shape[1]
    mask = mask_s[...]
    block = rows // sets
    stride = block // TILE - 1
    starts = [pl.multiple_of(step * stride + u * block, TILE) for u in range(sets)]
    fences = []
    for u in range(sets):
        same = ridc_ref[0, u] == ridr_ref[0, u]
        fences.append(jnp.where(same, 0.0, MASKED))
    for pair in range(0, groups, 2):
        units = [(u, g) for u in range(sets) for g in range(pair, pair + 2)]
        scores = []
        for u, g in units:
            here, cols = pl.ds(starts[u], COVER), pl.ds(g * lanes, lanes)
            scores.append(dot_rt(q_ref[here, cols], tiled(k_ref[here, cols], mask)))
        weights = []
        for (u, g), s in zip(units, scores):
            s = s + bias_s[step, g] + fences[u]
            parts = []
            for c in range(GROUP // 2):
                x = s[:, c * 2 * COVER : (c + 1) * 2 * COVER]
                top0 = jnp.max(jnp.where(low_half, x, MASKED), axis=1, keepdims=True)
                top1 = jnp.max(jnp.where(low_half, MASKED, x), axis=1, keepdims=True)
                top = jnp.maximum(jnp.where(low_half, top0, top1), MASKED * 0.1)
                parts.append(jnp.exp(x - top).astype(BF16))
            w = jnp.concatenate(parts, axis=1)
            p_ref[0, u, g] = w
            weights.append(w)
        mixed = []
        for (u, g), w in zip(units, weights):
            here, cols = pl.ds(starts[u], COVER), pl.ds(g * lanes, lanes)
            vals = jnp.concatenate([tiled(v_ref[here, cols], mask), mask], axis=1)
            mixed.append(dot(w, vals))
        for (u, g), a in zip(units, mixed):
            here, cols = pl.ds(starts[u], COVER), pl.ds(g * lanes, lanes)
            total = a[:, lanes:]
            inv = jnp.where(total > 0.0, 1.0 / jnp.maximum(total, 0.5), 0.0)
            att_ref[here, cols] += (a[:, :lanes] * inv).astype(BF16)
            rinv_ref[here, cols] += inv.astype(BF16)


def attn_rows(mid, w, qb, tab, idx, ridc, ridr, head_dim):
    rows, width = mid.shape
    heads = width // head_dim
    groups = heads // GROUP
    steps, sets = ridc.shape[0], ridc.shape[1]
    wide = GROUP * COVER
    row_out = jax.ShapeDtypeStruct((rows, width), BF16)
    return call(
        functools.partial(attn_kernel, head_dim),
        steps,
        (mid, w, qb, tab, idx, ridc, ridr),
        [
            whole(mid.shape),
            whole(w.shape),
            whole(qb.shape),
            whole(tab.shape),
            whole(idx.shape),
            pl.BlockSpec((1,) + ridc.shape[1:], lambda i: (i, 0, 0, 0)),
            pl.BlockSpec((1,) + ridr.shape[1:], lambda i: (i, 0, 0, 0)),
        ],
        [row_out] * 5 + [jax.ShapeDtypeStruct((steps, sets, groups, COVER, wide), BF16)],
        [whole((rows, width))] * 5
        + [pl.BlockSpec((1, sets, groups, COVER, wide), lambda i: (i, 0, 0, 0, 0))],
        [
            pltpu.VMEM((3 * width, width), BF16),
            pltpu.VMEM((heads, COVER, COVER), F32),
            pltpu.VMEM((TILE, groups, COVER, wide), F32),
            pltpu.VMEM((wide, GROUP * head_dim), BF16),
        ],
        2 * rows * width * 3 * width * 6,
        rows * width * 20,
    )


def gelu_parts(x):
    t = 1.0 / (1.0 + (0.3275911 / math.sqrt(2.0)) * jnp.abs(x))
    bell = jnp.exp(-0.5 * (x * x))
    poly = 0.5 * 1.061405429 * t + 0.5 * -1.453152027
    poly = poly * t + 0.5 * 1.421413741
    poly = poly * t + 0.5 * -0.284496736
    poly = poly * t + 0.5 * 0.254829592
    tail = poly * t * bell
    cdf = jnp.where(x > 0.0, 1.0 - tail, tail)
    return cdf, x * bell * (1.0 / math.sqrt(2.0 * math.pi))


def live_rows(limits_ref, start, count, micro_rows, width):
    row = lax.broadcasted_iota(jnp.int32, (count, width), 0) + start
    live = None
    for m in range(limits_ref.shape[1]):
        inside = (row >= m * micro_rows) & (row < m * micro_rows + limits_ref[0, m])
        live = inside if live is None else live | inside
    return live


def ffn_kernel(
    limits_ref,
    merged_ref,
    att_ref,
    cot_ref,
    rinv_ref,
    wp_ref,
    vecs_ref,
    ub_ref,
    up_ref,
    down_ref,
    out_ref,
    gmid_ref,
    gatt_ref,
    gffn_ref,
    gub_ref,
    gproj_ref,
    sums_ref,
    n2_s,
    inv_s,
    n_s,
    go_s,
    nt_s,
    gt_s,
    act_s,
    gp_s,
):
    chunk = pl.program_id(0)
    last = pl.num_programs(0) - 1
    rows, width = merged_ref.shape
    padded = n_s.shape[0]
    micro_rows = rows // limits_ref.shape[1]
    blocks = spans(rows, 512)

    @pl.when(chunk == 0)
    def _():
        bias_proj, gain2, bias2, bias_down = (vecs_ref[i : i + 1, :] for i in range(4))
        act_s[rows:, :] = jnp.zeros_like(act_s[rows:, :])
        gp_s[rows:, :] = jnp.zeros_like(gp_s[rows:, :])
        down_sum = jnp.zeros((1, width), F32)
        for start, count in blocks:
            here = pl.ds(start, count)
            middle = merged_ref[here, :] + dot(att_ref[here, :], wp_ref[...]) + bias_proj
            out_ref[here, :] = middle + bias_down
            normed, inverse = norm_parts(middle)
            n2_s[here, :] = normed.astype(BF16)
            inv_s[here, :] = jnp.broadcast_to(inverse, (count, inv_s.shape[1]))
            normed_ffn = (normed * gain2 + bias2).astype(BF16)
            n_s[here, :] = normed_ffn
            live = live_rows(limits_ref, start, count, micro_rows, width)
            grad_out = jnp.where(live, cot_ref[here, :].astype(F32), 0.0)
            down_sum = down_sum + jnp.sum(grad_out, axis=0, keepdims=True)
            grad_low = grad_out.astype(BF16)
            go_s[here, :] = grad_low
            whole_count = -(-count // 128) * 128
            if whole_count != count:
                filler = jnp.zeros((whole_count - count, width), BF16)
                normed_ffn = jnp.concatenate([normed_ffn, filler], axis=0)
                grad_low = jnp.concatenate([grad_low, filler], axis=0)
            nt_s[:, start : start + whole_count] = normed_ffn.T
            gt_s[:, start : start + whole_count] = grad_low.T
        sums_ref[...] = jnp.zeros_like(sums_ref)
        sums_ref[3:4, :] = down_sum
        gmid_ref[...] = jnp.zeros_like(gmid_ref)

    up_t, down = up_ref[0], down_ref[0]
    up_bias = ub_ref[0]
    up_sum = jnp.zeros((1, up_t.shape[0]), F32)
    for start, count in blocks:
        here = pl.ds(start, count)
        pre = dot_rt(n_s[here, :], up_t) + up_bias
        cdf, slope = gelu_parts(pre)
        act = (pre * cdf).astype(BF16)
        grad_pre = dot_rt(go_s[here, :], down) * (cdf + slope)
        up_sum = up_sum + jnp.sum(grad_pre, axis=0, keepdims=True)
        grad_pre = grad_pre.astype(BF16)
        act_s[here, :] = act
        gp_s[here, :] = grad_pre
        out_ref[here, :] += dot(act, down)
        gmid_ref[here, :] += dot(grad_pre, up_t)
    gub_ref[0] = up_sum
    hidden = up_t.shape[0]
    gffn_ref[0, :, :hidden] = dot(nt_s[...], gp_s[...]).astype(BF16)
    gffn_ref[0, :, hidden:] = dot(gt_s[...], act_s[...]).astype(BF16)

    @pl.when(chunk == last)
    def _():
        gain2 = vecs_ref[1:2, :]
        gain_sum = jnp.zeros((1, width), F32)
        bias_sum = jnp.zeros((1, width), F32)
        proj_sum = jnp.zeros((1, width), F32)
        gproj_ref[...] = jnp.zeros_like(gproj_ref)
        for start, count in blocks:
            here = pl.ds(start, count)
            live = live_rows(limits_ref, start, count, micro_rows, width)
            out_ref[here, :] = jnp.where(live, out_ref[here, :], 0.0)
            grad_ffn = gmid_ref[here, :]
            normed = n2_s[here, :].astype(F32)
            gain_sum = gain_sum + jnp.sum(grad_ffn * normed, axis=0, keepdims=True)
            bias_sum = bias_sum + jnp.sum(grad_ffn, axis=0, keepdims=True)
            grad_middle = go_s[here, :].astype(F32) + norm_back(
                grad_ffn * gain2, normed, inv_s[here, :1]
            )
            gmid_ref[here, :] = grad_middle
            proj_sum = proj_sum + jnp.sum(grad_middle, axis=0, keepdims=True)
            grad_attn = grad_middle.astype(BF16)
            gproj_ref[...] += dot_lt(att_ref[here, :], grad_attn)
            grad_att = dot_rt(grad_attn, wp_ref[...]) * rinv_ref[here, :].astype(F32)
            gatt_ref[here, :] = grad_att.astype(BF16)
        sums_ref[0:1, :] = proj_sum
        sums_ref[1:2, :] = gain_sum
        sums_ref[2:3, :] = bias_sum


def ffn_rows(limits, merged, att, cot, rinv, wp, vecs, ub, up, down):
    rows, width = merged.shape
    shards, hidden = up.shape[0], up.shape[1]
    padded = -(-rows // 128) * 128
    return call(
        ffn_kernel,
        shards,
        (limits, merged, att, cot, rinv, wp, vecs, ub, up, down),
        [
            pl.BlockSpec(memory_space=pltpu.SMEM),
            whole(merged.shape),
            whole(att.shape),
            whole(cot.shape),
            whole(rinv.shape),
            whole(wp.shape),
            whole(vecs.shape),
            pl.BlockSpec((1, 1, hidden), lambda i: (i, 0, 0)),
            pl.BlockSpec((1, hidden, width), lambda i: (i, 0, 0)),
            pl.BlockSpec((1, hidden, width), lambda i: (i, 0, 0)),
        ],
        [
            jax.ShapeDtypeStruct((rows, width), F32),
            jax.ShapeDtypeStruct((rows, width), F32),
            jax.ShapeDtypeStruct((rows, width), BF16),
            jax.ShapeDtypeStruct((shards, width, 2 * hidden), BF16),
            jax.ShapeDtypeStruct((shards, 1, hidden), F32),
            jax.ShapeDtypeStruct((width, width), F32),
            jax.ShapeDtypeStruct((8, width), F32),
        ],
        [
            whole((rows, width)),
            whole((rows, width)),
            whole((rows, width)),
            pl.BlockSpec((1, width, 2 * hidden), lambda i: (i, 0, 0)),
            pl.BlockSpec((1, 1, hidden), lambda i: (i, 0, 0)),
            whole((width, width)),
            whole((8, width)),
        ],
        [
            pltpu.VMEM((rows, width), BF16),
            pltpu.VMEM((rows, 128), F32),
            pltpu.VMEM((padded, width), BF16),
            pltpu.VMEM((padded, width), BF16),
            pltpu.VMEM((width, padded), BF16),
            pltpu.VMEM((width, padded), BF16),
            pltpu.VMEM((padded, hidden), BF16),
            pltpu.VMEM((padded, hidden), BF16),
        ],
        2 * rows * width * hidden * shards * 6,
        rows * width * 20,
    )


def attn_back_kernel(
    head_dim,
    q_ref,
    k_ref,
    v_ref,
    ga_ref,
    att_ref,
    p_ref,
    idx_ref,
    gq_ref,
    gk_ref,
    gv_ref,
    gtab_ref,
    ds_s,
    base_s,
    mask_s,
):
    step = pl.program_id(0)
    last = pl.num_programs(0) - 1
    rows, width = q_ref.shape
    lanes = GROUP * head_dim
    groups = width // lanes
    scale = 1.0 / math.sqrt(head_dim)
    sets = p_ref.shape[1]
    block = rows // sets

    @pl.when(step == 0)
    def _():
        mask_s[...] = head_mask(head_dim)
        gq_ref[...] = jnp.zeros_like(gq_ref)
        gk_ref[...] = jnp.zeros_like(gk_ref)
        gv_ref[...] = jnp.zeros_like(gv_ref)

    mask = mask_s[...]
    minus = -mask
    starts = [pl.multiple_of(step * (block // TILE - 1) + u * block, TILE) for u in range(sets)]
    lane_head = lax.broadcasted_iota(jnp.int32, (COVER, 2 * lanes), 1) % lanes // head_dim
    zeros = jnp.zeros((COVER, lanes), BF16)
    units = [(u, g) for g in range(groups) for u in range(sets)]

    def at(ref, u, g):
        return ref[pl.ds(starts[u], COVER), pl.ds(g * lanes, lanes)]

    grads = []
    for u, g in units:
        ga = at(ga_ref, u, g)
        left = jnp.concatenate([ga, ga * at(att_ref, u, g)], axis=1)
        right = jnp.concatenate([tiled(at(v_ref, u, g), mask), minus], axis=1)
        grads.append(dot_rt(left, right))
    score_grads = []
    totals = {}
    for (u, g), grad in zip(units, grads):
        ds = p_ref[0, u, g].astype(F32) * grad
        totals[g] = ds if g not in totals else totals[g] + ds
        score_grads.append(ds.astype(BF16))
    for g in range(groups):
        ds_s[step, g] = totals[g]
    query_grads = []
    for (u, g), ds in zip(units, score_grads):
        query_grads.append(dot(ds, tiled(at(k_ref, u, g), mask)))
    pair_grads = []
    for (u, g), ds in zip(units, score_grads):
        left = jnp.concatenate([ds, p_ref[0, u, g]], axis=0)
        right = jnp.concatenate(
            [
                jnp.concatenate([at(q_ref, u, g), zeros], axis=1),
                jnp.concatenate([zeros, at(ga_ref, u, g)], axis=1),
            ],
            axis=0,
        )
        pair_grads.append(dot_lt(left, right))
    for (u, g), grad_q, grad_kv in zip(units, query_grads, pair_grads):
        here, cols = pl.ds(starts[u], COVER), pl.ds(g * lanes, lanes)
        gq_ref[here, cols] += (grad_q * scale).astype(BF16)
        both = jnp.where(lane_head == 0, grad_kv[:COVER], 0.0)
        for h in range(1, GROUP):
            both = jnp.where(lane_head == h, grad_kv[h * COVER : (h + 1) * COVER], both)
        both = both.astype(BF16)
        gk_ref[here, cols] += both[:, :lanes]
        gv_ref[here, cols] += both[:, lanes:]

    @pl.when(step == last)
    def _():
        for g in range(groups):

            def unshift(o, acc):
                turned = pltpu.roll(ds_s[o, g], COVER - o, 0)
                return acc + pltpu.roll(turned, GROUP * COVER - o, 1)

            full = lax.fori_loop(0, TILE, unshift, jnp.zeros((COVER, GROUP * COVER), F32))
            for h in range(GROUP):
                base_s[g * GROUP + h] = full[:, h * COVER : (h + 1) * COVER]
        grad = jnp.zeros(gtab_ref.shape, F32)
        for pair in range(idx_ref.shape[0]):
            row = idx_ref[pair : pair + 1, :]
            vals = jnp.concatenate([base_s[:, 2 * pair, :], base_s[:, 2 * pair + 1, :]], axis=1)
            onehot = index_onehot(row, grad.shape[1])
            high = vals.astype(BF16)
            grad = grad + dot_rt(high, onehot)
            grad = grad + dot_rt((vals - high.astype(F32)).astype(BF16), onehot)
        gtab_ref[...] = grad


def attn_back_rows(q, k, v, ga, att, p, idx, table_width, head_dim):
    rows, width = q.shape
    heads = width // head_dim
    steps, sets, groups, _, wide = p.shape
    row_out = jax.ShapeDtypeStruct((rows, width), BF16)
    return call(
        functools.partial(attn_back_kernel, head_dim),
        steps,
        (q, k, v, ga, att, p, idx),
        [whole((rows, width))] * 5
        + [
            pl.BlockSpec((1, sets, groups, COVER, wide), lambda i: (i, 0, 0, 0, 0)),
            whole(idx.shape),
        ],
        [row_out] * 3 + [jax.ShapeDtypeStruct((heads, table_width), F32)],
        [whole((rows, width))] * 3 + [whole((heads, table_width))],
        [
            pltpu.VMEM((TILE, groups, COVER, wide), F32),
            pltpu.VMEM((heads, COVER, COVER), F32),
            pltpu.VMEM((wide, GROUP * head_dim), BF16),
        ],
        2 * rows * width * 3 * width * 6,
        rows * width * 20,
    )


def dense_back_kernel(
    head_dim,
    gq_ref,
    gk_ref,
    gv_ref,
    mid_ref,
    merged_ref,
    gmid_ref,
    w_ref,
    x_ref,
    g1_ref,
    gm_ref,
    gqkv_ref,
    gqb_ref,
    gmerge_ref,
    sums_ref,
    wt_s,
):
    step = pl.program_id(0)
    width = mid_ref.shape[1]
    grad_refs = (gq_ref, gk_ref, gv_ref)

    @pl.when(step == 0)
    def _():
        shards, local = w_ref.shape[0], w_ref.shape[1] // (3 * head_dim)
        for s in range(shards):
            for l in range(local):
                for t in range(3):
                    at = t * width + (s * local + l) * head_dim
                    wt_s[at : at + head_dim, :] = w_ref[
                        s, (3 * l + t) * head_dim : (3 * l + t + 1) * head_dim, :
                    ]
        gqkv_ref[...] = jnp.zeros_like(gqkv_ref)
        gqb_ref[...] = jnp.zeros_like(gqb_ref)
        gmerge_ref[...] = jnp.zeros_like(gmerge_ref)
        sums_ref[...] = jnp.zeros_like(sums_ref)

    mid_t = mid_ref[...].T
    grad_mid = None
    for t in range(3):
        grad = grad_refs[t][...]
        gqkv_ref[:, t * width : (t + 1) * width] += dot(mid_t, grad)
        gqb_ref[:, t * width : (t + 1) * width] += jnp.sum(
            grad.astype(F32), axis=0, keepdims=True
        )
        part = dot(grad, wt_s[t * width : (t + 1) * width, :])
        grad_mid = part if grad_mid is None else grad_mid + part
    normed1, inverse1 = norm_parts(merged_ref[...])
    sums_ref[0:1, :] += jnp.sum(grad_mid * normed1, axis=0, keepdims=True)
    sums_ref[1:2, :] += jnp.sum(grad_mid, axis=0, keepdims=True)
    grad_merged = gmid_ref[...] + norm_back(grad_mid * g1_ref[...], normed1, inverse1)
    sums_ref[2:3, :] += jnp.sum(grad_merged, axis=0, keepdims=True)
    grad_merged = grad_merged.astype(BF16)
    gm_ref[...] = grad_merged
    normed0, _ = norm_parts(x_ref[...].astype(F32))
    gmerge_ref[...] += dot_lt(grad_merged, normed0.astype(BF16))


def dense_back_rows(gq, gk, gv, mid, merged, gmid, w, x, g1, head_dim):
    rows, width = mid.shape
    wide = x.shape[1]
    step = rows // 3
    row_block = pl.BlockSpec((step, width), lambda i: (i, 0))
    return call(
        functools.partial(dense_back_kernel, head_dim),
        3,
        (gq, gk, gv, mid, merged, gmid, w, x, g1),
        [row_block] * 6
        + [
            whole(w.shape),
            pl.BlockSpec((step, wide), lambda i: (i, 0)),
            whole(g1.shape),
        ],
        [
            jax.ShapeDtypeStruct((rows, width), BF16),
            jax.ShapeDtypeStruct((width, 3 * width), F32),
            jax.ShapeDtypeStruct((1, 3 * width), F32),
            jax.ShapeDtypeStruct((width, wide), F32),
            jax.ShapeDtypeStruct((8, width), F32),
        ],
        [
            row_block,
            whole((width, 3 * width)),
            whole((1, 3 * width)),
            whole((width, wide)),
            whole((8, width)),
        ],
        [pltpu.VMEM((3 * width, width), BF16)],
        2 * rows * width * (6 * width + wide),
        rows * width * 20,
    )


def input_back_kernel(gm_ref, wm_ref, x_ref, g0_ref, out_ref):
    grad_low = dot_rt(gm_ref[...], wm_ref[...])
    normed, inverse = norm_parts(x_ref[...].astype(F32))
    out_ref[...] = norm_back(grad_low * g0_ref[...], normed, inverse)


def input_back_rows(gm, wm, x, g0):
    rows, width = gm.shape
    wide = x.shape[1]
    step = rows // 7
    return call(
        input_back_kernel,
        7,
        (gm, wm, x, g0),
        [
            pl.BlockSpec((step, width), lambda i: (i, 0)),
            whole(wm.shape),
            pl.BlockSpec((step, wide), lambda i: (i, 0)),
            whole(g0.shape),
        ],
        jax.ShapeDtypeStruct((rows, wide), F32),
        pl.BlockSpec((step, wide), lambda i: (i, 0)),
        [],
        2 * rows * width * wide,
        rows * wide * 7,
    )


def swap(block, axis, bit, size):
    return lax.ppermute(block, axis, [(i, i ^ bit) for i in range(size)])


def bits_of(size):
    return [1 << i for i in range(size.bit_length() - 1)]


def gather_relative(own, axis, size):
    blocks = {0: own}
    for bit in reversed(bits_of(size)):
        have = sorted(blocks)
        sent = jnp.stack([blocks[r] for r in have])
        came = swap(sent, axis, bit, size)
        for i, r in enumerate(have):
            blocks[r ^ bit] = came[i]
    return jnp.stack([blocks[r] for r in range(size)])


def scatter_sum(parts, axis, size):
    held = parts
    for bit in bits_of(size):
        halves = held.reshape((held.shape[0] // 2, 2) + held.shape[1:])
        came = swap(halves[:, 1], axis, bit, size)
        held = halves[:, 0] + came
    return held[0]


def total_sum(block, axis, size):
    for bit in bits_of(size):
        block = block + swap(block, axis, bit, size)
    return block


def shards(
    inputs,
    norm0_gain,
    norm0_bias,
    merge_weight,
    norm1_gain,
    norm1_bias,
    qkv_weight,
    qkv_bias,
    rel_table,
    rel_index,
    regions,
    live_windows,
    proj_weight,
    proj_bias,
    norm2_gain,
    norm2_bias,
    up_weight,
    up_bias,
    down_weight,
    down_bias,
    cotangent,
    n_dp,
    n_mp,
):
    micro, strip_rows, wide = inputs.shape
    width = merge_weight.shape[1]
    win = rel_index.shape[0]
    local, packed = qkv_bias.shape
    head_dim = packed // 3
    heads = local * n_mp
    hidden = up_bias.shape[0]
    rel = rel_table.shape[1]
    rows = micro * strip_rows
    windows = rows // win
    sets = windows // TILE
    strip = lax.axis_index("mp")

    small = jnp.zeros((TILE, width), BF16)
    small = small.at[:local, :packed].set(qkv_bias)
    small = small.at[:local, packed : packed + rel].set(rel_table)
    small = small.at[local, :hidden].set(up_bias)
    first = jnp.concatenate(
        [jnp.transpose(qkv_weight, (1, 2, 0)).reshape(local * packed, width), small], axis=0
    )
    first = gather_relative(first, "mp", n_mp)
    second = jnp.concatenate(
        [proj_weight.reshape(local * head_dim, width), up_weight.T, down_weight], axis=0
    )
    second = gather_relative(second, "mp", n_mp)
    qkv_all = first[:, : local * packed]
    small_all = first[:, local * packed :].astype(F32)
    bias_all = small_all[:, :local, :packed].reshape(heads, 3, head_dim)
    bias_all = jnp.transpose(bias_all, (1, 0, 2)).reshape(1, 3 * width)
    table_width = -(-rel // 128) * 128
    table = small_all[:, :local, packed : packed + rel].reshape(heads, rel)
    table = jnp.pad(table, ((0, 0), (0, table_width - rel))).astype(BF16)
    up_bias_all = small_all[:, local, :hidden].reshape(n_mp, 1, hidden)
    proj_all = second[:, : local * head_dim].reshape(width, width)
    up_all = second[:, local * head_dim : local * head_dim + hidden]
    down_all = second[:, local * head_dim + hidden :]

    index = jnp.pad(rel_index, ((0, win % 2), (0, COVER - win)), constant_values=-1)
    index = index.reshape(-1, 2 * COVER)
    region = lax.dynamic_slice_in_dim(regions, strip * strip_rows, strip_rows, axis=1)
    region = jnp.pad(region.reshape(sets, TILE, win), ((0, 0), (0, 0), (0, COVER - win)))
    region = jnp.stack([jnp.roll(region[:, o], o, axis=1) for o in range(TILE)])
    region_col = region[..., None]
    region_row = jnp.tile(region[:, :, None, :], (1, 1, 1, GROUP))
    strip_windows = strip_rows // win
    limits = jnp.clip(live_windows[:, 0] - strip * strip_windows, 0, strip_windows) * win
    limits = limits.reshape(1, micro).astype(jnp.int32)

    x = inputs.reshape(rows, wide)
    merged, mid = merge_rows(
        x, norm0_gain[None], norm0_bias[None], merge_weight, norm1_gain[None], norm1_bias[None]
    )
    q, k, v, att, rinv, p = attn_rows(
        mid, qkv_all, bias_all, table, index, region_col, region_row, head_dim
    )
    vecs = jnp.stack([proj_bias, norm2_gain, norm2_bias, down_bias] + [down_bias] * 4)
    out, gmid, gatt, gffn, gub, gproj, sums2 = ffn_rows(
        limits,
        merged,
        att,
        cotangent.reshape(rows, width),
        rinv,
        proj_all,
        vecs,
        up_bias_all,
        up_all,
        down_all,
    )
    ffn_part = scatter_sum(gffn, "mp", n_mp)
    ffn_part = total_sum(ffn_part, "dp", n_dp).astype(F32)
    gq, gk, gv, gtab = attn_back_rows(q, k, v, gatt, att, p, index, table_width, head_dim)
    gm, gqkv, gqb, gmerge, sums1 = dense_back_rows(
        gq, gk, gv, mid, merged, gmid, qkv_all, x, norm1_gain[None], head_dim
    )
    grad_input = input_back_rows(gm, merge_weight, x, norm0_gain[None])

    gqkv = jnp.transpose(gqkv.astype(BF16).reshape(width, 3, heads, head_dim), (2, 1, 3, 0))
    gqkv = gqkv.reshape(n_mp, local * packed, width)
    gproj = gproj.astype(BF16).reshape(n_mp, local * head_dim, width)
    gqb = jnp.transpose(gqb.reshape(3, heads, head_dim), (1, 0, 2)).reshape(n_mp, local, packed)
    gtab = gtab[:, :rel].reshape(n_mp, local, rel)
    tail = jnp.zeros((n_mp, TILE, width), BF16)
    tail = tail.at[:, :local, :packed].set(gqb.astype(BF16))
    tail = tail.at[:, :local, packed : packed + rel].set(gtab.astype(BF16))
    tail = tail.at[:, local, :hidden].set(gub[:, 0].astype(BF16))
    part = jnp.concatenate([gqkv, gproj, tail], axis=1)
    part = total_sum(scatter_sum(part, "mp", n_mp), "dp", n_dp).astype(F32)
    gqkv = jnp.transpose(part[: local * packed].reshape(local, packed, width), (2, 0, 1))
    gproj = part[local * packed : local * (packed + head_dim)].reshape(local, head_dim, width)
    tail = part[local * (packed + head_dim) :]
    sums = jnp.concatenate([sums2[:4], sums1[:4]], axis=0)
    sums = total_sum(total_sum(sums, "mp", n_mp), "dp", n_dp)
    gmerge = total_sum(total_sum(gmerge.astype(BF16), "mp", n_mp), "dp", n_dp)
    gmerge = gmerge.astype(F32).T
    low_sum = sums[6]
    wide_weight = merge_weight.astype(F32)
    grad_gain0 = jnp.sum(wide_weight * gmerge, axis=1)
    grad_bias0 = jnp.sum(wide_weight * low_sum[None], axis=1)
    gmerge = gmerge * norm0_gain[:, None] + norm0_bias[:, None] * low_sum[None]
    return (
        out.reshape(micro, strip_rows, width),
        grad_input.reshape(micro, strip_rows, wide),
        grad_gain0,
        grad_bias0,
        gmerge,
        sums[4],
        sums[5],
        gqkv,
        tail[:local, :packed],
        tail[:local, packed : packed + rel],
        gproj,
        sums[0],
        sums[1],
        sums[2],
        ffn_part[:, :hidden],
        tail[local, :hidden],
        ffn_part[:, hidden:].T,
        sums[3],
    )


def solution(mesh):
    placed = (
        P(None, ("dp", "mp"), None),
        P(),
        P(),
        P(),
        P(),
        P(),
        P(None, "mp", None),
        P("mp", None),
        P("mp", None),
        P(),
        P(None, "dp"),
        P(None, "dp"),
        P("mp", None, None),
        P(),
        P(),
        P(),
        P(None, "mp"),
        P("mp"),
        P("mp", None),
        P(),
        P(None, ("dp", "mp"), None),
    )
    return jax.shard_map(
        functools.partial(shards, n_dp=mesh.shape["dp"], n_mp=mesh.shape["mp"]),
        mesh=mesh,
        in_specs=placed,
        out_specs=(
            P(None, ("dp", "mp"), None),
            P(None, ("dp", "mp"), None),
            P(),
            P(),
            P(),
            P(),
            P(),
            P(None, "mp", None),
            P("mp", None),
            P("mp", None),
            P("mp", None, None),
            P(),
            P(),
            P(),
            P(None, "mp"),
            P("mp"),
            P("mp", None),
            P(),
        ),
        check_vma=False,
    )
```

time: 1160 us -> 485 us (0.42); the launches traced: 1140 us -> 478 us
  local copies, waits for them, and re-layouts: 367 us -> 54.5 us
  matrix products: 298 us -> 0 us
  Pallas kernels: 0 us -> 186 us
  blocking collectives: 140 us -> 0 us
  other arithmetic: 95.6 us -> 31.6 us
  between operations: 16.8 us -> 1.68 us
    dot_general x44 -> x0, matrix products: 298 us -> none  [the longest x10 81.8 us: matmul(): return jnp.dot(left, right, preferred_element_type=jnp.float32)]
    pallas_call x0 -> x6, Pallas kernels: none -> 186 us  [call(): pl.pallas_call(kernel, grid=(grid,), in_specs=in_specs, out_specs=out_spe...]
    ppermute x0 -> x26, waiting for transfers between devices: none -> 175 us  [swap(): return lax.ppermute(block, axis, [(i, i ^ bit) for i in range(size)])]
    unnamed x205 -> x66, local copies, waits for them, and re-layouts: 113 us -> 18.5 us
    psum x2 -> x0, waiting for transfers between devices: 89 us -> none  [the longest x1 89 us: shards(): lax.psum((grad_merge, grad_norm0_gain, grad_norm0_bias, grad_norm1_gain,...]
    all_gather x3 -> x0, blocking collectives: 78 us -> none  [the longest x1 56.9 us: shards(): lax.all_gather(up_bias, 'mp', axis=0, tiled=True)]
    all_to_all x8 -> x0, local copies, waits for them, and re-layouts: 74.3 us -> none  [the longest x2 23.3 us: shards(): lax.all_to_all(packed, 'mp', split_axis=1, concat_axis=0, tiled=True)]
    all_to_all x8 -> x0, waiting for transfers between devices: 60.8 us -> none  [the longest x2 38.6 us: shards(): lax.all_to_all(packed, 'mp', split_axis=1, concat_axis=0, tiled=True)]
  transfers between devices with their start and end apart: 17 -> 26, of which waited for: 6 -> 12; matrix products, arithmetic and copies ran while one was open for 59% -> 10% of each run, Pallas kernels for 0% -> 24%
where the time goes in v1:
time: 485 us; the launch traced here: 478 us
  Pallas kernels  186 us (38%)
  waiting for transfers between devices  175 us (36%)
  local copies, waits for them, and re-layouts  54.5 us (11%)
  other arithmetic  31.6 us (7%)
  starting transfers between devices  29.1 us (6%)
    pallas_call x6, Pallas kernels, call(): pl.pallas_call(kernel, grid=(grid,), in_specs=in_specs, out_specs=out_spe...  186 us
    ppermute x26, waiting for transfers between devices, swap(): return lax.ppermute(block, axis, [(i, i ^ bit) for i in range(size)])  175 us
    ppermute x26, starting transfers between devices, swap(): return lax.ppermute(block, axis, [(i, i ^ bit) for i in range(size)])  29.1 us
    unnamed x66, local copies, waits for them, and re-layouts  18.5 us
  transfers between devices with their start and end apart: 26, of which 12 were waited for; matrix products, arithmetic and copies ran while one was open for 10% of the time, Pallas kernels for 24%

profile of v1, /device:TPU:0, one launch (start us, length us, event | category | flops | bytes accessed | tf_op | source)
XLA Modules:
  0.0 478.0 jit_solution(3418923294484271559)
XLA Ops:
  3.9 2.7 broadcast_select_fusion.1
  6.6 2.0 scatter.21
  9.8 3.0 collective-permute-start
  19.0 2.1 collective-permute-start.1
  22.1 7.2 %collective-permute-done.1 = bf16[2,208,512]{2,1,0:T(8,128)(2,1)S(1)} collective-permute-done((bf16[2,208,512]{2,1,0:T(8,128)(2,1)S(1)}, bf16[2,208,512]{2,1,0:T(8,128)(2,1)S(1)}, u32[]{:S(2)}, u32[]{:S(2)}) %collective-permute-start.1) | collective-permute-done | bytes 426016 | tf_op jit(solution)/shard_map/ppermute | solution.py:709
  35.8 10.3 %shard_map.340 = (f32[2352,512]{1,0:T(8,128)}, bf16[2352,512]{1,0:T(8,128)(2,1)}) custom-call(bf16[2352,1024]{1,0:T(8,128)(2,1)} %bitcast.240, f32[1,1024]{1,0:T(1,128)} %bitcast.282, f32[1,1024]{1,0:T(1,128)} %bitcast.285, bf16[1024,512]{1,0:T(8,128)(2,1)} %wm_ref.3, f32[1,512]{1,0:T(1,128)} %bitcast.298, f32[1,512]{1,0:T(1,128)} %bitcast.297), custom_call_target="tpu_custom_call" | custom-call | flops 2466250752 | bytes 12042240 | tf_op jit(solution)/shard_map/pallas_call | solution.py:38
  50.6 24.1 %collective-permute-done.4 = bf16[2,576,512]{2,1,0:T(8,128)(2,1)S(1)} collective-permute-done((bf16[2,576,512]{2,1,0:T(8,128)(2,1)S(1)}, bf16[2,576,512]{2,1,0:T(8,128)(2,1)S(1)}, u32[]{:S(2)}, u32[]{:S(2)}) %collective-permute-start.4) | collective-permute-done | bytes 1179680 | tf_op jit(solution)/shard_map/ppermute | solution.py:709
  80.8 37.0 %shard_map.341 = (bf16[2352,512]{1,0:T(8,128)(2,1)}, bf16[2352,512]{1,0:T(8,128)(2,1)}, bf16[2352,512]{1,0:T(8,128)(2,1)}, bf16[2352,512]{1,0:T(8,128)(2,1)}, bf...) custom-call(bf16[2352,512]{1,0:T(8,128)(2,1)} %get-tuple-element.115.mid_ref, ...), custom_call_target="tpu_custom_call" | custom-call | flops 22196256768 | bytes 24084480 | tf_op jit(solution)/shard_map/pallas_call | solution.py:38
  117.8 1.9 slice_dynamic-update-slice_fusion.3
  128.0 4.6 fusion.14
  134.5 69.5 %shard_map.342 = (f32[2352,512]{1,0:T(8,128)}, f32[2352,512]{1,0:T(8,128)}, bf16[2352,512]{1,0:T(8,128)(2,1)}, bf16[8,512,512]{2,1,0:T(8,128)(2,1)}, f32[8,1,256...) custom-call(s32[1,2]{1,0:T(1,128)} %multiply_bitcast_fusion.limits_ref, ...), custom_call_target="tpu_custom_call" | custom-call | flops 29595009024 | bytes 24084480 | tf_op jit(solution)/shard_map/pallas_call | solution.py:38
  203.9 3.1 slice_bitcast_fusion
  207.5 35.0 %shard_map.343 = (bf16[2352,512]{1,0:T(8,128)(2,1)}, bf16[2352,512]{1,0:T(8,128)(2,1)}, bf16[2352,512]{1,0:T(8,128)(2,1)}, f32[16,256]{1,0:T(8,128)}) custom-call(bf16[2352,512]{1,0:T(8,128)(2,1)} %get-tuple-element.119.q_ref, bf16[2352,512]{1,0:T(8,128)(2,1)} %get-tuple-element.120.k_ref, bf16[2352,512]{1,0:T(8,128)(2,1)} %get-tuple-element.121.v_ref, ...), custom_call_target="tpu_custom_call" | custom-call | flops 22196256768 | bytes 24084480 | tf_op jit(solution)/shard_map/pallas_call | solution.py:38
  242.5 23.0 %shard_map.344 = (bf16[2352,512]{1,0:T(8,128)(2,1)}, f32[512,1536]{1,0:T(8,128)}, f32[1,1536]{1,0:T(1,128)}, f32[512,1024]{1,0:T(8,128)}, f32[8,512]{1,0:T(8,128)}) custom-call(bf16[2352,512]{1,0:T(8,128)(2,1)} %get-tuple-element.124.gq_ref, bf16[2352,512]{1,0:T(8,128)(2,1)} %get-tuple-element.125.gk_ref, bf16[2352,512]{1,0:T(8,128)(2,1)} %get-tuple-element.126.gv_ref, ...), custom_call_target="tpu_custom_call" | custom-call | flops 9865003008 | bytes 24084480 | tf_op jit(solution)/shard_map/pallas_call | solution.py:38
  265.6 2.7 convert_element_type.47
  269.4 2.1 convert_element_type.48
  273.4 2.0 broadcast_select_fusion
  275.5 4.2 scatter.26
  285.2 2.0 fusion.2
  288.0 21.7 %collective-permute-done.7 = bf16[512,1024]{1,0:T(8,128)(2,1)S(1)} collective-permute-done((bf16[512,1024]{1,0:T(8,128)(2,1)S(1)}, bf16[512,1024]{1,0:T(8,128)(2,1)S(1)}, u32[]{:S(2)}, u32[]{:S(2)}) %collective-permute-start.7) | collective-permute-done | bytes 1048608 | tf_op jit(solution)/shard_map/ppermute | solution.py:709
  313.2 18.9 %collective-permute-done.22 = bf16[2,512,512]{2,1,0:T(8,128)(2,1)S(1)} collective-permute-done((bf16[2,512,512]{2,1,0:T(8,128)(2,1)S(1)}, bf16[2,512,512]{2,1,0:T(8,128)(2,1)S(1)}, u32[]{:S(2)}, u32[]{:S(2)}) %collective-permute-start.22) | collective-permute-done | bytes 1048608 | tf_op jit(solution)/shard_map/ppermute | solution.py:709
  333.8 9.9 %collective-permute-done.17 = bf16[2,272,512]{2,1,0:T(8,128)(2,1)S(1)} collective-permute-done((bf16[2,272,512]{2,1,0:T(8,128)(2,1)S(1)}, bf16[2,272,512]{2,1,0:T(8,128)(2,1)S(1)}, u32[]{:S(2)}, u32[]{:S(2)}) %collective-permute-start.17) | collective-permute-done | bytes 557088 | tf_op jit(solution)/shard_map/ppermute | solution.py:709
  348.8 5.1 %collective-permute-done.18 = bf16[1,272,512]{2,1,0:T(8,128)(2,1)S(1)} collective-permute-done((bf16[1,272,512]{2,1,0:T(8,128)(2,1)S(1)}, bf16[1,272,512]{2,1,0:T(8,128)(2,1)S(1)}, u32[]{:S(2)}, u32[]{:S(2)}) %collective-permute-start.18) | collective-permute-done | bytes 278560 | tf_op jit(solution)/shard_map/ppermute | solution.py:709
  356.0 2.3 collective-permute-done.12
  359.7 2.3 collective-permute-done.13
  364.9 21.8 %collective-permute-done.14 = f32[8,512]{1,0:T(8,128)S(1)} collective-permute-done((f32[8,512]{1,0:T(8,128)S(1)}, f32[8,512]{1,0:T(8,128)S(1)}, u32[]{:S(2)}, u32[]{:S(2)}) %collective-permute-start.14) | collective-permute-done | bytes 16416 | tf_op jit(solution)/shard_map/ppermute | solution.py:709
  386.6 2.5 collective-permute-start.15
  391.3 2.6 collective-permute-start.10
  395.7 11.5 %shard_map.345 = f32[2352,1024]{1,0:T(8,128)} custom-call(bf16[2352,512]{1,0:T(8,128)(2,1)} %get-tuple-element.128.gm_ref, bf16[1024,512]{1,0:T(8,128)(2,1)} %wm_ref.3, bf16[2352,1024]{1,0:T(8,128)(2,1)} %bitcast.242, f32[1,1024]{1,0:T(1,128)} %bitcast.283), custom_call_target="tpu_custom_call" | custom-call | flops 2466250752 | bytes 16859136 | tf_op jit(solution)/shard_map/pallas_call | solution.py:38
  407.8 30.2 %collective-permute-done.20 = bf16[272,512]{1,0:T(8,128)(2,1)S(1)} collective-permute-done((bf16[272,512]{1,0:T(8,128)(2,1)S(1)}, bf16[272,512]{1,0:T(8,128)(2,1)S(1)}, u32[]{:S(2)}, u32[]{:S(2)}) %collective-permute-start.20) | collective-permute-done | bytes 278560 | tf_op jit(solution)/shard_map/ppermute | solution.py:709
  441.3 29.6 %collective-permute-done.25 = bf16[512,512]{1,0:T(8,128)(2,1)S(1)} collective-permute-done((bf16[512,512]{1,0:T(8,128)(2,1)S(1)}, bf16[512,512]{1,0:T(8,128)(2,1)S(1)}, u32[]{:S(2)}, u32[]{:S(2)}) %collective-permute-start.25) | collective-permute-done | bytes 524320 | tf_op jit(solution)/shard_map/ppermute | solution.py:709
  472.8 3.0 fusion.1
  (225 shorter events, 76.6 us)
Async XLA Ops:
  0.7 14.4 %copy-start = (s32[2,9408]{1,0:T(2,128)S(1)}, s32[2,9408]{1,0:T(2,128)}, u32[]{:S(2)}) copy-start(s32[2,9408]{1,0:T(2,128)} %param.43) | copy-start | bytes 225796
  0.7 20.7 %copy-start.8 = (bf16[512,2,96]{0,2,1:T(8,128)(2,1)S(1)}, bf16[512,2,96]{0,2,1:T(8,128)(2,1)}, u32[]{:S(2)}) copy-start(bf16[512,2,96]{0,2,1:T(8,128)(2,1)} %param.39) | copy-start | bytes 589828
  9.8 9.1 %collective-permute-start = (bf16[1,208,512]{2,1,0:T(8,128)(2,1)S(1)}, bf16[1,208,512]{2,1,0:T(8,128)(2,1)S(1)}, u32[]{:S(2)}, u32[]{:S(2)}) collective-permute-start(bf16[1,208,512]{2,1,0:T(8,128)(2,1)S(1)} %maximum_bitcast_fusion.1), channel_id=1, source_target_pairs={{0,4},{1,5},{2,6},{3,7},{4,0},{5,1},{6,2},{7,3},{8,12},{9,13},{10,... | collective-permute-start | bytes 638984 | tf_op jit(solution)/shard_map/ppermute | solution.py:709
  15.0 31.2 %collective-permute-start.3 = (bf16[1,576,512]{2,1,0:T(8,128)(2,1)S(1)}, bf16[1,576,512]{2,1,0:T(8,128)(2,1)S(1)}, u32[]{:S(2)}, u32[]{:S(2)}) collective-permute-start(bf16[1,576,512]{2,1,0:T(8,128)(2,1)S(1)} %maximum_bitcast_fusion), channel_id=1, source_target_pairs={{0,4},{1,5},{2,6},{3,7},{4,0},{5,1},{6,2},{7,3},{8,12},{9,13},{10,... | collective-permute-start | bytes 1769480 | tf_op jit(solution)/shard_map/ppermute | solution.py:709
  19.0 10.2 %collective-permute-start.1 = (bf16[2,208,512]{2,1,0:T(8,128)(2,1)S(1)}, bf16[2,208,512]{2,1,0:T(8,128)(2,1)S(1)}, u32[]{:S(2)}, u32[]{:S(2)}) collective-permute-start(bf16[2,208,512]{2,1,0:T(8,128)(2,1)S(1)} %pad_maximum_fusion.4), channel_id=1, source_target_pairs={{0,2},{1,3},{2,0},{3,1},{4,6},{5,7},{6,4},{7,5},{8,10},{9,11},{10,... | collective-permute-start | bytes 1277960 | tf_op jit(solution)/shard_map/ppermute | solution.py:709
  22.1 12.4 %copy-start.7 = (bf16[256,512]{1,0:T(8,128)(2,1)S(1)}, bf16[256,512]{1,0:T(8,128)(2,1)}, u32[]{:S(2)}) copy-start(bf16[256,512]{1,0:T(8,128)(2,1)} %param.51) | copy-start | bytes 786436
  30.3 17.4 %collective-permute-start.2 = (bf16[4,208,512]{2,1,0:T(8,128)(2,1)}, bf16[4,208,512]{2,1,0:T(8,128)(2,1)}, u32[]{:S(2)}, u32[]{:S(2)}) collective-permute-start(bf16[4,208,512]{2,1,0:T(8,128)(2,1)} %pad_maximum_fusion.3), channel_id=1, source_target_pairs={{0,1},{1,0},{2,3},{3,2},{4,5},{5,4},{6,7},{7,6},{8,9},{9,8},{10,11... | collective-permute-start | bytes 2555912 | tf_op jit(solution)/shard_map/ppermute | solution.py:709
  46.2 28.4 %collective-permute-start.4 = (bf16[2,576,512]{2,1,0:T(8,128)(2,1)S(1)}, bf16[2,576,512]{2,1,0:T(8,128)(2,1)S(1)}, u32[]{:S(2)}, u32[]{:S(2)}) collective-permute-start(bf16[2,576,512]{2,1,0:T(8,128)(2,1)S(1)} %pad_maximum_fusion.2), channel_id=1, source_target_pairs={{0,2},{1,3},{2,0},{3,1},{4,6},{5,7},{6,4},{7,5},{8,10},{9,11},{10,... | collective-permute-start | bytes 3538952 | tf_op jit(solution)/shard_map/ppermute | solution.py:709
  76.4 41.4 %collective-permute-start.5 = (bf16[4,576,512]{2,1,0:T(8,128)(2,1)}, bf16[4,576,512]{2,1,0:T(8,128)(2,1)}, u32[]{:S(2)}, u32[]{:S(2)}) collective-permute-start(bf16[4,576,512]{2,1,0:T(8,128)(2,1)} %pad_maximum_fusion), channel_id=1, source_target_pairs={{0,1},{1,0},{2,3},{3,2},{4,5},{5,4},{6,7},{7,6},{8,9},{9,8},{10,11... | collective-permute-start | bytes 7077896 | tf_op jit(solution)/shard_map/ppermute | solution.py:709
  207.0 78.2 %collective-permute-start.21 = (bf16[4,512,512]{2,1,0:T(8,128)(2,1)}, bf16[4,512,512]{2,1,0:T(8,128)(2,1)}, u32[]{:S(2)}, u32[]{:S(2)}) collective-permute-start(bf16[4,512,512]{2,1,0:T(8,128)(2,1)} %slice_bitcast_fusion), channel_id=1, source_target_pairs={{0,1},{1,0},{2,3},{3,2},{4,5},{5,4},{6,7},{7,6},{8,9},{9,8},{10,11... | collective-permute-start | bytes 6291464 | tf_op jit(solution)/shard_map/ppermute | solution.py:709
  268.3 12.8 %collective-permute-start.6 = (bf16[512,1024]{1,0:T(8,128)(2,1)}, bf16[512,1024]{1,0:T(8,128)(2,1)}, u32[]{:S(2)}, u32[]{:S(2)}) collective-permute-start(bf16[512,1024]{1,0:T(8,128)(2,1)} %convert_element_type.47), channel_id=1, source_target_pairs={{0,1},{1,0},{2,3},{3,2},{4,5},{5,4},{6,7},{7,6},{8,9},{9,8},{10,11... | collective-permute-start | bytes 3145736 | tf_op jit(solution)/shard_map/ppermute | solution.py:709
  280.5 7.3 %collective-permute-start.16 = (bf16[4,272,512]{2,1,0:T(8,128)(2,1)S(1)}, bf16[4,272,512]{2,1,0:T(8,128)(2,1)S(1)}, u32[]{:S(2)}, u32[]{:S(2)}) collective-permute-start(bf16[4,272,512]{2,1,0:T(8,128)(2,1)S(1)} %slice_bitcast_fusion.2), channel_id=1, source_target_pairs={{0,1},{1,0},{2,3},{3,2},{4,5},{5,4},{6,7},{7,6},{8,9},{9,8},{10,11... | collective-permute-start | bytes 3342344 | tf_op jit(solution)/shard_map/ppermute | solution.py:709
  283.7 26.0 %collective-permute-start.7 = (bf16[512,1024]{1,0:T(8,128)(2,1)S(1)}, bf16[512,1024]{1,0:T(8,128)(2,1)S(1)}, u32[]{:S(2)}, u32[]{:S(2)}) collective-permute-start(bf16[512,1024]{1,0:T(8,128)(2,1)S(1)} %convert_add_fusion), channel_id=1, source_target_pairs={{0,2},{1,3},{2,0},{3,1},{4,6},{5,7},{6,4},{7,5},{8,10},{9,11},{10,... | collective-permute-start | bytes 3145736 | tf_op jit(solution)/shard_map/ppermute | solution.py:709
  287.2 45.0 %collective-permute-start.22 = (bf16[2,512,512]{2,1,0:T(8,128)(2,1)S(1)}, bf16[2,512,512]{2,1,0:T(8,128)(2,1)S(1)}, u32[]{:S(2)}, u32[]{:S(2)}) collective-permute-start(bf16[2,512,512]{2,1,0:T(8,128)(2,1)S(1)} %slice_bitcast_fusion.4), channel_id=1, source_target_pairs={{0,2},{1,3},{2,0},{3,1},{4,6},{5,7},{6,4},{7,5},{8,10},{9,11},{10,... | collective-permute-start | bytes 3145736 | tf_op jit(solution)/shard_map/ppermute | solution.py:709
  310.1 33.7 %collective-permute-start.8 = (bf16[512,1024]{1,0:T(8,128)(2,1)S(1)}, bf16[512,1024]{1,0:T(8,128)(2,1)S(1)}, u32[]{:S(2)}, u32[]{:S(2)}) collective-permute-start(bf16[512,1024]{1,0:T(8,128)(2,1)S(1)} %add.90), channel_id=1, source_target_pairs={{0,4},{1,5},{2,6},{3,7},{4,0},{5,1},{6,2},{7,3},{8,12},{9,13},{10,... | collective-permute-start | bytes 3145736 | tf_op jit(solution)/shard_map/ppermute | solution.py:709
  311.6 22.2 %copy-start.17 = (f32[8,512]{1,0:T(8,128)S(1)}, f32[8,512]{1,0:T(8,128)}, u32[]{:S(2)}) copy-start(f32[8,512]{1,0:T(8,128)} %get-tuple-element.131) | copy-start | bytes 49156
  311.7 22.2 %copy-start.16 = (f32[8,512]{1,0:T(8,128)S(1)}, f32[8,512]{1,0:T(8,128)}, u32[]{:S(2)}) copy-start(f32[8,512]{1,0:T(8,128)} %get-tuple-element.130) | copy-start | bytes 49156
  311.7 32.0 %collective-permute-start.17 = (bf16[2,272,512]{2,1,0:T(8,128)(2,1)S(1)}, bf16[2,272,512]{2,1,0:T(8,128)(2,1)S(1)}, u32[]{:S(2)}, u32[]{:S(2)}) collective-permute-start(bf16[2,272,512]{2,1,0:T(8,128)(2,1)S(1)} %slice_bitcast_fusion.6), channel_id=1, source_target_pairs={{0,2},{1,3},{2,0},{3,1},{4,6},{5,7},{6,4},{7,5},{8,10},{9,11},{10,... | collective-permute-start | bytes 1671176 | tf_op jit(solution)/shard_map/ppermute | solution.py:709
  332.3 15.1 %collective-permute-start.23 = (bf16[1,512,512]{2,1,0:T(8,128)(2,1)S(1)}, bf16[1,512,512]{2,1,0:T(8,128)(2,1)S(1)}, u32[]{:S(2)}, u32[]{:S(2)}) collective-permute-start(bf16[1,512,512]{2,1,0:T(8,128)(2,1)S(1)} %slice_bitcast_fusion.9), channel_id=1, source_target_pairs={{0,4},{1,5},{2,6},{3,7},{4,0},{5,1},{6,2},{7,3},{8,12},{9,13},{10,... | collective-permute-start | bytes 1572872 | tf_op jit(solution)/shard_map/ppermute | solution.py:709
  344.2 19.4 %copy-start.4 = (bf16[1024,512]{1,0:T(8,128)(2,1)S(1)}, bf16[1024,512]{1,0:T(8,128)(2,1)}, u32[]{:S(2)}) copy-start(bf16[1024,512]{1,0:T(8,128)(2,1)} %wm_ref.3) | copy-start | bytes 3145732
  344.2 45.5 %collective-permute-start.9 = (bf16[512,1024]{1,0:T(8,128)(2,1)S(1)}, bf16[512,1024]{1,0:T(8,128)(2,1)}, u32[]{:S(2)}, u32[]{:S(2)}) collective-permute-start(bf16[512,1024]{1,0:T(8,128)(2,1)S(1)} %add.91), channel_id=1, source_target_pairs={{0,8},{8,0},{16,24},{24,16},{1,9},{9,1},{17,25},{25,17},{2,10},{10... | collective-permute-start | bytes 3145736 | tf_op jit(solution)/shard_map/ppermute | solution.py:709
  345.8 8.1 %collective-permute-start.18 = (bf16[1,272,512]{2,1,0:T(8,128)(2,1)S(1)}, bf16[1,272,512]{2,1,0:T(8,128)(2,1)S(1)}, u32[]{:S(2)}, u32[]{:S(2)}) collective-permute-start(bf16[1,272,512]{2,1,0:T(8,128)(2,1)S(1)} %slice_bitcast_fusion.11), channel_id=1, source_target_pairs={{0,4},{1,5},{2,6},{3,7},{4,0},{5,1},{6,2},{7,3},{8,12},{9,13},{10,... | collective-permute-start | bytes 835592 | tf_op jit(solution)/shard_map/ppermute | solution.py:709
  348.2 45.7 %collective-permute-start.24 = (bf16[512,512]{1,0:T(8,128)(2,1)}, bf16[512,512]{1,0:T(8,128)(2,1)}, u32[]{:S(2)}, u32[]{:S(2)}) collective-permute-start(bf16[512,512]{1,0:T(8,128)(2,1)} %fusion.10), channel_id=1, source_target_pairs={{0,8},{8,0},{16,24},{24,16},{1,9},{9,1},{17,25},{25,17},{2,10},{10... | collective-permute-start | bytes 1572872 | tf_op jit(solution)/shard_map/ppermute | solution.py:709
  348.7 5.8 %collective-permute-start.11 = (f32[8,512]{1,0:T(8,128)S(1)}, f32[8,512]{1,0:T(8,128)S(1)}, u32[]{:S(2)}, u32[]{:S(2)}) collective-permute-start(f32[8,512]{1,0:T(8,128)S(1)} %pad_maximum_fusion.5), channel_id=1, source_target_pairs={{0,1},{1,0},{2,3},{3,2},{4,5},{5,4},{6,7},{7,6},{8,9},{9,8},{10,11... | collective-permute-start | bytes 49160 | tf_op jit(solution)/shard_map/ppermute | solution.py:709
  353.9 35.2 %collective-permute-start.19 = (bf16[272,512]{1,0:T(8,128)(2,1)S(1)}, bf16[272,512]{1,0:T(8,128)(2,1)S(1)}, u32[]{:S(2)}, u32[]{:S(2)}) collective-permute-start(bf16[272,512]{1,0:T(8,128)(2,1)S(1)} %fusion.12), channel_id=1, source_target_pairs={{0,8},{8,0},{16,24},{24,16},{1,9},{9,1},{17,25},{25,17},{2,10},{10... | collective-permute-start | bytes 835592 | tf_op jit(solution)/shard_map/ppermute | solution.py:709
  354.5 3.8 collective-permute-start.12
  358.3 3.7 collective-permute-start.13
  362.1 24.6 %collective-permute-start.14 = (f32[8,512]{1,0:T(8,128)S(1)}, f32[8,512]{1,0:T(8,128)S(1)}, u32[]{:S(2)}, u32[]{:S(2)}) collective-permute-start(f32[8,512]{1,0:T(8,128)S(1)} %add.96), channel_id=1, source_target_pairs={{0,8},{8,0},{16,24},{24,16},{1,9},{9,1},{17,25},{25,17},{2,10},{10... | collective-permute-start | bytes 49160 | tf_op jit(solution)/shard_map/ppermute | solution.py:709
  386.6 20.6 %collective-permute-start.15 = (f32[8,512]{1,0:T(8,128)S(1)}, f32[8,512]{1,0:T(8,128)S(1)}, u32[]{:S(2)}, u32[]{:S(2)}) collective-permute-start(f32[8,512]{1,0:T(8,128)S(1)} %add.97), channel_id=1, source_target_pairs={{0,16},{8,24},{16,0},{24,8},{1,17},{9,25},{17,1},{25,9},{2,18},{10... | collective-permute-start | bytes 49160 | tf_op jit(solution)/shard_map/ppermute | solution.py:709
  389.2 48.8 %collective-permute-start.20 = (bf16[272,512]{1,0:T(8,128)(2,1)S(1)}, bf16[272,512]{1,0:T(8,128)(2,1)S(1)}, u32[]{:S(2)}, u32[]{:S(2)}) collective-permute-start(bf16[272,512]{1,0:T(8,128)(2,1)S(1)} %add.103), channel_id=1, source_target_pairs={{0,16},{8,24},{16,0},{24,8},{1,17},{9,25},{17,1},{25,9},{2,18},{10... | collective-permute-start | bytes 835592 | tf_op jit(solution)/shard_map/ppermute | solution.py:709
  391.3 81.5 %collective-permute-start.10 = (bf16[512,1024]{1,0:T(8,128)(2,1)S(1)}, bf16[512,1024]{1,0:T(8,128)(2,1)}, u32[]{:S(2)}, u32[]{:S(2)}) collective-permute-start(bf16[512,1024]{1,0:T(8,128)(2,1)S(1)} %add.92), channel_id=1, source_target_pairs={{0,16},{8,24},{16,0},{24,8},{1,17},{9,25},{17,1},{25,9},{2,18},{10... | collective-permute-start | bytes 3145736 | tf_op jit(solution)/shard_map/ppermute | solution.py:709
  395.3 75.6 %collective-permute-start.25 = (bf16[512,512]{1,0:T(8,128)(2,1)S(1)}, bf16[512,512]{1,0:T(8,128)(2,1)S(1)}, u32[]{:S(2)}, u32[]{:S(2)}) collective-permute-start(bf16[512,512]{1,0:T(8,128)(2,1)S(1)} %add.108), channel_id=1, source_target_pairs={{0,16},{8,24},{16,0},{24,8},{1,17},{9,25},{17,1},{25,9},{2,18},{10... | collective-permute-start | bytes 1572872 | tf_op jit(solution)/shard_map/ppermute | solution.py:709
  (18 other events, 104.9 us)
